TPU v7x, 128 devices: a whole 4x4x4 slice. The times are simulated.
128 devices in a mesh: req: 16 (over z, y), head: 8 (over x, core).
Axes of the slice: x: 4, y: 4, z: 4, core: 2. Of those that a mesh axis runs over, the one named last changes fastest.
Arguments:
- queries: bfloat16 [256, 64, 8192], P('req', None, 'head'), may hold values from -6 to 6
- keys: bfloat16 [256, 64, 8192], P('req', None, 'head'), may hold values from -1.5 to 1.5
- values: bfloat16 [256, 64, 8192], P('req', None, 'head'), may hold values from -6 to 6
- states: float32 [256, 64, 128, 128], P('req', 'head'), may hold values from -3 to 3
- parents: int32 [256, 64], P('req'), may hold values from -1 to 62, as said below
- path_nodes: int32 [256, 64], P('req'), may hold values from -1 to 63, as said below
- held: int32 [256], replicated, may hold values from 0 to 255, as said below
- rates: float32 [64], P('head'), may hold values from 0.004 to 0.15
- gain: float32 [8192], P('head'), may hold values from 0.5 to 2
Outputs:
- mixed: bfloat16 [256, 64, 8192], P('req', None, 'head')
- new_states: float32 [256, 64, 128, 128], P('req', 'head')
Inputs may be any that keep to these rules, and one draw needn't show every extreme that they name: `parents`: node 0 has parent -1; every other node's parent is a lower-numbered node. `path_nodes`: a row lists the accepted path from node 0 down the tree, each entry a child of the one before, then -1 to the end. `held`: a permutation of the requests; each aligned block of 16 rows holds exactly 1 request of every aligned block of 16 requests.
All inputs are finite; a program needn't handle non-finite values.
Results may differ from a plain program's by a relative error of at most 0.0056.
Values may be sent and summed in bfloat16 or wider, within the bound.
No kernel may reach another device: no remote copies, remote signals or barrier semaphores. Data moves between devices by JAX's collectives and lax.ppermute only.
A program may use at most 128 MiB of HBM per device.

v0:
```python
import jax
import jax.numpy as jnp
from jax import lax
from jax.sharding import PartitionSpec as P

HEADS = 64
HD = 128


EPS = 1e-06
HIGH = lax.Precision.HIGHEST


def ancestry(parents):
    nodes = parents.shape[-1]
    column = jnp.arange(nodes, dtype=jnp.int32)
    step_map = (parents[:, :, None] == column[None, None, :]).astype(jnp.float32)
    reach = jnp.broadcast_to(jnp.eye(nodes, dtype=jnp.float32), step_map.shape)
    for repeat in range(nodes.bit_length()):
        grown = lax.optimization_barrier(
            jnp.einsum("rij,rjk->rik", step_map, reach, precision=HIGH)
        )
        reach = reach + grown
        step_map = jnp.einsum("rij,rjk->rik", step_map, step_map, precision=HIGH)
    return reach


def attend(queries, keys, values, parents, path_nodes, states, rates):
    rows, nodes, width = queries.shape
    heads = rates.shape[0]
    size = width // heads
    q_heads = queries.reshape(rows, nodes, heads, size)
    k_heads = keys.reshape(rows, nodes, heads, size)
    v_heads = values.reshape(rows, nodes, heads, size)
    reach = ancestry(parents)
    depth = jnp.sum(reach, axis=-1)
    column = jnp.arange(nodes, dtype=jnp.int32)
    onpath = jnp.sum((path_nodes[:, :, None] == column[None, None, :]).astype(jnp.float32), axis=1)
    length = jnp.sum((path_nodes >= 0).astype(jnp.float32), axis=1)
    spacing = jnp.maximum(depth[:, :, None] - depth[:, None, :], 0.0)
    fading = jnp.exp(-rates[None, :, None, None] * spacing[:, None]) * reach[:, None]
    scores = jnp.einsum("rnhd,rmhd->rhnm", q_heads, k_heads, preferred_element_type=jnp.float32)
    weights = (scores * fading).astype(jnp.bfloat16)
    local = lax.optimization_barrier(
        jnp.einsum("rhnm,rmhd->rnhd", weights, v_heads, preferred_element_type=jnp.float32)
    )
    prior = lax.optimization_barrier(
        jnp.einsum("rnhd,rhde->rnhe", q_heads.astype(jnp.float32), states, precision=HIGH)
    )
    prior = prior * jnp.exp(-rates[None, None, :, None] * depth[:, :, None, None])
    attn = (local + prior).astype(jnp.bfloat16).reshape(rows, nodes, width)
    leading = jnp.exp(-rates[None, :] * length[:, None])
    path_weight = onpath[:, None, :] * jnp.exp(
        -rates[None, :, None] * (length[:, None, None] - depth[:, None, :])
    )
    scaled_keys = k_heads.astype(jnp.float32) * jnp.transpose(path_weight, (0, 2, 1))[:, :, :, None]
    update = lax.optimization_barrier(
        jnp.einsum("rnhd,rnhe->rhde", scaled_keys, v_heads.astype(jnp.float32), precision=HIGH)
    )
    fresh = leading[:, :, None, None] * states + update
    return (attn, fresh)


def body(queries, keys, values, states, parents, path_nodes, held, rates, gain):
    req_count = lax.axis_size("req")
    req_rank = lax.axis_index("req")
    per_dev = queries.shape[0]
    per_pair = per_dev // req_count
    positions = jnp.arange(per_dev, dtype=jnp.int32)
    table = held.reshape(req_count, per_dev)
    sources = table // per_dev
    marked = jnp.where(sources == req_rank, 0, 1) * per_dev + positions[None, :]
    picked = jnp.argsort(marked, axis=1)[:, :per_pair]
    send_ids = (jnp.take_along_axis(table, picked, axis=1) - req_rank * per_dev).reshape(-1)
    own_row = lax.dynamic_index_in_dim(table, req_rank, 0, keepdims=False)
    order = jnp.argsort(own_row // per_dev * per_dev + positions)
    placing = jnp.argsort(order)
    restore = jnp.argsort(send_ids)
    fetched = (
        lax.all_to_all(states[order], "req", split_axis=0, concat_axis=0, tiled=True),
        lax.all_to_all(
            parents[order].astype(jnp.float32), "req", split_axis=0, concat_axis=0, tiled=True
        ),
        lax.all_to_all(
            path_nodes[order].astype(jnp.float32), "req", split_axis=0, concat_axis=0, tiled=True
        ),
    )
    attn_sent, fresh_sent = attend(
        queries[send_ids],
        keys[send_ids],
        values[send_ids],
        fetched[1].astype(jnp.int32),
        fetched[2].astype(jnp.int32),
        fetched[0],
        rates,
    )
    fresh_back = lax.all_to_all(fresh_sent, "req", split_axis=0, concat_axis=0, tiled=True)
    new_states = fresh_back[placing]
    attn = attn_sent[restore]
    attn_wide = attn.astype(jnp.float32)
    partial_value = jnp.sum(attn_wide * attn_wide, axis=-1)
    total = lax.psum(partial_value, "head")
    scaling = lax.rsqrt(total / (HEADS * HD) + EPS)
    mixed = (attn_wide * scaling[:, :, None] * gain).astype(jnp.bfloat16)
    return (mixed, new_states)


def solution(mesh):
    in_specs = (
        P("req", None, "head"),
        P("req", None, "head"),
        P("req", None, "head"),
        P("req", "head", None, None),
        P("req", None),
        P("req", None),
        P(),
        P("head"),
        P("head"),
    )
    out_specs = (P("req", None, "head"), P("req", "head", None, None))
    return jax.shard_map(body, mesh=mesh, in_specs=in_specs, out_specs=out_specs, check_vma=False)
```

profile of v0, /device:TPU:0, one launch (start us, length us, event | category | flops | bytes accessed | tf_op | source)
XLA Modules:
  0.0 301.0 jit_solution(7368652694045539220)
XLA Ops:
  0.6 0.0 copy-start
  0.7 0.9 reshape.144
  1.6 1.2 sort.63
  2.8 1.3 gather_fusion.3
  4.1 0.6 convert_element_type.76
  4.7 8.1 %all-to-all-start = ((f32[16,1,64]{2,1,0:T(1,128)}), f32[16,1,64]{2,1,0:T(1,128)S(1)}, u32[]{:S(2)}, u32[]{:S(2)}) async-start(f32[16,1,64]{2,1,0:T(1,128)} %bitcast.7), calls=%async_computation | async-start | bytes 16384 | tf_op jit(solution)/shard_map/all_to_all | solution.py:81
  12.8 1.3 gather_fusion.6
  14.1 0.6 convert_element_type.84
  14.7 5.6 %all-to-all-done = f32[16,1,64]{2,1,0:T(1,128)S(1)} async-done(((f32[16,1,64]{2,1,0:T(1,128)}), f32[16,1,64]{2,1,0:T(1,128)S(1)}, u32[]{:S(2)}, u32[]{:S(2)}) %all-to-all-start) | async-done | bytes 4128 | tf_op jit(solution)/shard_map/all_to_all | solution.py:81
  20.3 3.5 %all-to-all-start.2 = ((f32[16,1,64]{2,1,0:T(1,128)}), f32[16,1,64]{2,1,0:T(1,128)S(1)}, u32[]{:S(2)}, u32[]{:S(2)}) async-start(f32[16,1,64]{2,1,0:T(1,128)} %bitcast.13), calls=%async_computation.2 | async-start | bytes 16384 | tf_op jit(solution)/shard_map/all_to_all | solution.py:84
  23.8 7.9 %gather_fusion.4 = f32[16,8,128,128]{3,2,1,0:T(8,128)} fusion(f32[16,8,128,128]{3,2,1,0:T(8,128)} %param.12, s32[1024]{0:T(1024)S(1)} %pad_clamp_fusion.2), kind=kCustom, calls=%fused_computation.4 | custom fusion | bytes 16777280 | tf_op jit(solution)/shard_map/gather | solution.py:80
  31.7 0.0 all-to-all-done.2
  31.7 7.3 %all-to-all-start.1 = ((f32[16,8,128,128]{3,2,1,0:T(8,128)}), f32[16,8,128,128]{3,2,1,0:T(8,128)}, u32[]{:S(2)}, u32[]{:S(2)}) async-start(f32[16,8,128,128]{3,2,1,0:T(8,128)} %gather_fusion.4), calls=%async_computation.1 | async-start | bytes 16777216 | tf_op jit(solution)/shard_map/all_to_all | solution.py:80
  39.0 0.0 copy-done.6
  39.1 0.1 copy.31
  39.2 0.7 sort.62
  39.9 0.7 gather_fusion.8
  40.6 2.0 gather_fusion
  42.6 3.6 %gather_fusion.2 = bf16[16,64,1024]{2,1,0:T(8,128)(2,1)} fusion(bf16[16,64,1024]{2,1,0:T(8,128)(2,1)} %param.10, s32[1024]{0:T(1024)S(1)} %pad_clamp_fusion.3), kind=kCustom, calls=%fused_computation.2 | custom fusion | bytes 4194368 | tf_op jit(solution)/shard_map/gather | solution.py:90
  46.2 0.5 fusion.25
  46.7 0.7 fusion.24
  47.3 0.7 fusion.26
  48.0 0.6 fusion.43
  48.6 0.7 fusion.33
  49.3 0.6 fusion.44
  50.0 0.1 fusion.32
  50.1 0.6 fusion.45
  50.7 0.1 add.83
  50.8 0.6 fusion.46
  51.5 0.6 fusion.47
  52.1 0.1 add.84
  52.2 0.6 fusion.48
  52.8 0.6 fusion.49
  53.5 0.1 add.85
  53.5 0.0 copy-start.2
  53.6 0.6 fusion.50
  54.2 0.6 fusion.51
  54.9 0.1 convert_reduce_fusion.1
  55.0 0.2 convert_reduce_fusion
  55.2 0.2 fusion.41
  55.4 0.1 broadcast_subtract_fusion
  55.5 0.1 exponential_multiply_fusion
  55.6 0.1 copy-done.3
  55.8 10.1 %fusion.3 = f32[16,8,128,128]{3,2,1,0:T(8,128)} fusion(f32[16,64,8]{1,2,0:T(8,128)S(1)} %get-tuple-element.14, bf16[16,64,1024]{2,1,0:T(8,128)(2,1)S(1)} %copy-done.2, bf16[16,64,1024]{2,1,0:T(8,128)(2,1)S(1)} %copy-done.3), kind=kOutput, calls=%fused_computation.15 | convolution fusion | flops 1612709888 | bytes 12615680 | tf_op jit(solution)/shard_map/rnhd,rnhe->rhde/dot_general | solution.py:58
  65.9 0.1 multiply_exponential_fusion.1
  66.0 93.8 %all-to-all-done.1 = f32[16,8,128,128]{3,2,1,0:T(8,128)} async-done(((f32[16,8,128,128]{3,2,1,0:T(8,128)}), f32[16,8,128,128]{3,2,1,0:T(8,128)}, u32[]{:S(2)}, u32[]{:S(2)}) %all-to-all-start.1) | async-done | bytes 8388640 | tf_op jit(solution)/shard_map/all_to_all | solution.py:80
  159.8 10.0 %multiply_add_fusion = f32[16,8,128,128]{3,2,1,0:T(8,128)} fusion(f32[16,8,128,128]{3,2,1,0:T(8,128)} %fusion.3, f32[16,8,128,128]{3,2,1,0:T(8,128)} %all-to-all-done.1, f32[16,8]{1,0:T(8,128)S(1)} %multiply_exponential_fusion.1), kind=kLoop, calls=%fused_computation.9 | loop fusion | flops 4194304 | bytes 25166336 | tf_op jit(solution)/shard_map/add | solution.py:60
  169.8 4.9 %all-to-all-start.3 = ((f32[16,8,128,128]{3,2,1,0:T(8,128)}), f32[16,8,128,128]{3,2,1,0:T(8,128)}, u32[]{:S(2)}, u32[]{:S(2)}) async-start(f32[16,8,128,128]{3,2,1,0:T(8,128)} %multiply_add_fusion), calls=%async_computation.3 | async-start | bytes 16777216 | tf_op jit(solution)/shard_map/all_to_all | solution.py:97
  174.7 2.3 gather_fusion.1
  177.0 1.2 sort.65
  178.3 1.2 sort.64
  179.6 0.2 subtract_maximum_fusion
  179.8 6.0 %convolution_bitcast_fusion = f32[16,64,8,128]{3,1,2,0:T(8,128)} fusion(f32[16,64,64]{2,1,0:T(8,128)S(1)} %get-tuple-element.11, f32[16,64,64]{2,1,0:T(8,128)S(1)} %subtract_maximum_fusion, f32[8]{0:T(128)S(1)} %neg.10, bf16[16,64,1024]{2,1,0:T(8,128)(2,1)} %gather_fusion, bf16[16,64,1024]{2,1,0:T(8,128)(2,1)} %gather_fusion.2, ...), kind=kOutput, calls=%fused_computation.20 | convolution fusion | flops 270532608 | bytes 11010080 | tf_op jit(solution)/shard_map/rhnm,rmhd->rnhd/dot_general | solution.py:45
  185.7 6.8 %convolution_bitcast_fusion.1 = f32[16,64,8,128]{3,1,2,0:T(8,128)S(1)} fusion(f32[16,8,128,128]{3,2,1,0:T(8,128)} %all-to-all-done.1, bf16[16,64,1024]{2,1,0:T(8,128)(2,1)S(1)} %gather_fusion.1), kind=kOutput, calls=%fused_computation.21 | convolution fusion | flops 1610612736 | bytes 14680064 | tf_op jit(solution)/shard_map/rnhd,rhde->rnhe/dot_general | solution.py:48
  192.5 0.0 copy-done.4
  192.5 2.4 copy_bitcast_fusion
  194.9 2.3 gather_fusion.5
  197.1 0.0 copy-start.5
  197.2 0.5 fusion
  197.6 13.5 %psum.7 = f32[16,64]{1,0:T(8,128)S(1)} all-reduce(f32[16,64]{1,0:T(8,128)S(1)} %fusion), channel_id=1, replica_groups=mesh['req'=16,'head'=8] {'head'}, use_global_device_ids=true, to_apply=%region_5.6 | all-reduce | flops 1024 | bytes 8192 | tf_op jit(solution)/shard_map/psum | solution.py:102
  211.1 1.9 fusion.2
  213.0 80.0 %all-to-all-done.3 = f32[16,8,128,128]{3,2,1,0:T(8,128)} async-done(((f32[16,8,128,128]{3,2,1,0:T(8,128)}), f32[16,8,128,128]{3,2,1,0:T(8,128)}, u32[]{:S(2)}, u32[]{:S(2)}) %all-to-all-start.3) | async-done | bytes 8388640 | tf_op jit(solution)/shard_map/all_to_all | solution.py:97
  293.0 8.0 %gather_fusion.7 = f32[16,8,128,128]{3,2,1,0:T(8,128)} fusion(f32[16,8,128,128]{3,2,1,0:T(8,128)} %all-to-all-done.3, s32[1024]{0:T(1024)S(1)} %pad_clamp_fusion), kind=kCustom, calls=%fused_computation.7 | custom fusion | bytes 16777280 | tf_op jit(solution)/shard_map/gather | solution.py:98
  301.0 0.0 copy-done.1
  (30 shorter events, 0.2 us)
Async XLA Ops:
  0.6 40.0 %copy-start = (bf16[16,64,1024]{2,1,0:T(8,128)(2,1)S(1)}, bf16[16,64,1024]{2,1,0:T(8,128)(2,1)}, u32[]{:S(2)}) copy-start(bf16[16,64,1024]{2,1,0:T(8,128)(2,1)} %param.11) | copy-start | bytes 6291460
  4.7 15.6 %all-to-all-start = ((f32[16,1,64]{2,1,0:T(1,128)}), f32[16,1,64]{2,1,0:T(1,128)S(1)}, u32[]{:S(2)}, u32[]{:S(2)}) async-start(f32[16,1,64]{2,1,0:T(1,128)} %bitcast.7), calls=%async_computation | async-start | bytes 16384 | tf_op jit(solution)/shard_map/all_to_all | solution.py:81
  20.3 11.4 %all-to-all-start.2 = ((f32[16,1,64]{2,1,0:T(1,128)}), f32[16,1,64]{2,1,0:T(1,128)S(1)}, u32[]{:S(2)}, u32[]{:S(2)}) async-start(f32[16,1,64]{2,1,0:T(1,128)} %bitcast.13), calls=%async_computation.2 | async-start | bytes 16384 | tf_op jit(solution)/shard_map/all_to_all | solution.py:84
  31.7 7.4 %copy-start.6 = (f32[8]{0:T(128)S(1)}, f32[8]{0:T(128)}, u32[]{:S(2)}) copy-start(f32[8]{0:T(128)} %param.16) | copy-start | bytes 100
  31.7 128.1 %all-to-all-start.1 = ((f32[16,8,128,128]{3,2,1,0:T(8,128)}), f32[16,8,128,128]{3,2,1,0:T(8,128)}, u32[]{:S(2)}, u32[]{:S(2)}) async-start(f32[16,8,128,128]{3,2,1,0:T(8,128)} %gather_fusion.4), calls=%async_computation.1 | async-start | bytes 16777216 | tf_op jit(solution)/shard_map/all_to_all | solution.py:80
  53.5 2.1 copy-start.2
  53.6 2.2 copy-start.3
  169.8 123.2 %all-to-all-start.3 = ((f32[16,8,128,128]{3,2,1,0:T(8,128)}), f32[16,8,128,128]{3,2,1,0:T(8,128)}, u32[]{:S(2)}, u32[]{:S(2)}) async-start(f32[16,8,128,128]{3,2,1,0:T(8,128)} %multiply_add_fusion), calls=%async_computation.3 | async-start | bytes 16777216 | tf_op jit(solution)/shard_map/all_to_all | solution.py:97
  185.7 6.8 %copy-start.4 = (f32[16,64,8,128]{3,1,2,0:T(8,128)S(1)}, f32[16,64,8,128]{3,1,2,0:T(8,128)}, u32[]{:S(2)}) copy-start(f32[16,64,8,128]{3,1,2,0:T(8,128)} %convolution_bitcast_fusion) | copy-start | bytes 12582916
  197.1 14.0 %copy-start.5 = (f32[1024]{0:T(1024)S(1)}, f32[1024]{0:T(1024)}, u32[]{:S(2)}) copy-start(f32[1024]{0:T(1024)} %param.17) | copy-start | bytes 12292
  293.0 8.0 %copy-start.1 = (bf16[16,64,1024]{2,1,0:T(8,128)(2,1)S(1)}, bf16[16,64,1024]{2,1,0:T(8,128)(2,1)}, u32[]{:S(2)}) copy-start(bf16[16,64,1024]{2,1,0:T(8,128)(2,1)} %param.11) | copy-start | bytes 6291460
where the time goes:
time: 302 us; the launch traced here: 301 us
  waiting for transfers between devices  179 us (59%)
  matrix products  31.1 us (10%)
  local copies, waits for them, and re-layouts  30.4 us (10%)
  starting transfers between devices  23.8 us (8%)
  other arithmetic  21.8 us (7%)
  blocking collectives  13.5 us (4%)
    all_to_all x1, waiting for transfers between devices, body(): lax.all_to_all(states[order], 'req', split_axis=0, concat_axis=0, tiled=T...  93.8 us
    all_to_all x1, waiting for transfers between devices, body(): lax.all_to_all(fresh_sent, 'req', split_axis=0, concat_axis=0, tiled=True)  80 us
    psum x1, blocking collectives, body(): total = lax.psum(partial_value, 'head')  13.5 us
    dot_general x1, matrix products, attend(): jnp.einsum('rnhd,rnhe->rhde', scaled_keys, v_heads.astype(jnp.float32), p...  10.1 us
    add x1, other arithmetic, attend(): fresh = leading[:, :, None, None] * states + update  10 us
    all_to_all x1, starting transfers between devices, body(): lax.all_to_all(parents[order].astype(jnp.float32), 'req', split_axis=0, c...  8.13 us
    gather x1, local copies, waits for them, and re-layouts, body(): new_states = fresh_back[placing]  8.01 us
    gather x1, local copies, waits for them, and re-layouts, body(): states[order]  7.86 us
  transfers between devices with their start and end apart: 4, of which 3 were waited for; matrix products, arithmetic and copies ran while one was open for 20% of the time, Pallas kernels for 0%

commit v1 on v0

v1 whole, which is shorter than its diff:
```python
import functools

import jax
import jax.numpy as jnp
from jax import lax
from jax.experimental import pallas as pl
from jax.experimental.pallas import tpu as pltpu
from jax.sharding import PartitionSpec as P

HEADS = 64
HD = 128
NODES = 64
EPS = 1e-06
F32 = jnp.float32
BF16 = jnp.bfloat16


def dot(a, b, dims=((1,), (0,))):
    return lax.dot_general(a, b, (dims, ((), ())), preferred_element_type=F32)


def cast_kernel(rows, dest_ref, states_ref, out_ref, wide, narrow, in_sem, out_sem):
    def fetch(j):
        return pltpu.make_async_copy(states_ref.at[j], wide.at[j], in_sem.at[j])

    def store(j):
        return pltpu.make_async_copy(narrow.at[j], out_ref.at[dest_ref[j]], out_sem.at[j])

    for j in range(rows):
        fetch(j).start()
    for j in range(rows):
        fetch(j).wait()
        narrow[j] = wide[j].astype(BF16)
        store(j).start()
    for j in range(rows):
        store(j).wait()


def cast_states(dest, states):
    rows, height, width = states.shape
    return pl.pallas_call(
        functools.partial(cast_kernel, rows),
        out_shape=jax.ShapeDtypeStruct(states.shape, BF16),
        in_specs=[
            pl.BlockSpec(memory_space=pltpu.SMEM),
            pl.BlockSpec(memory_space=pl.ANY),
        ],
        out_specs=pl.BlockSpec(memory_space=pl.ANY),
        scratch_shapes=[
            pltpu.VMEM(states.shape, F32),
            pltpu.VMEM(states.shape, BF16),
            pltpu.SemaphoreType.DMA((rows,)),
            pltpu.SemaphoreType.DMA((rows,)),
        ],
        compiler_params=pltpu.CompilerParams(vmem_limit_bytes=24 << 20),
        cost_estimate=pl.CostEstimate(flops=0, bytes_accessed=states.size * 6, transcendentals=0),
        name="cast_states",
    )(dest, states)


def tree_kernel(
    heads, ids_ref, pos_ref, rates_ref, tree_ref, q_ref, k_ref, v_ref, local_ref, update_ref, depth_ref
):
    tree = tree_ref[0]
    parents = tree[:, :NODES]
    path = tree[:, NODES:]
    row = lax.broadcasted_iota(jnp.int32, (NODES, NODES), 0)
    col = lax.broadcasted_iota(jnp.int32, (NODES, NODES), 1)
    step = (jnp.broadcast_to(parents, (NODES, NODES)) == row).astype(F32).astype(BF16)
    reach_t = (row == col).astype(F32) + step.astype(F32)
    hops = 2
    while hops < NODES:
        step = dot(step, step).astype(BF16)
        reach_t = reach_t + dot(step, reach_t.astype(BF16))
        hops *= 2
    depth_row = jnp.sum(reach_t, axis=0, keepdims=True)
    reach = reach_t.T
    depth = jnp.sum(reach, axis=1, keepdims=True)
    spacing = jnp.maximum(depth - depth_row, 0.0)
    onpath = jnp.sum(
        (jnp.broadcast_to(path, (NODES, NODES)) == row).astype(F32), axis=1, keepdims=True
    )
    length = jnp.sum((path >= 0).astype(F32), axis=1, keepdims=True)
    depth_ref[0] = jnp.broadcast_to(depth, (NODES, HD))
    for h in range(heads):
        at = slice(h * HD, (h + 1) * HD)
        rate = rates_ref[h]
        q, k, v = q_ref[0, :, at], k_ref[0, :, at], v_ref[0, :, at]
        fading = jnp.exp(-rate * spacing) * reach
        weights = (dot(q, k, ((1,), (1,))) * fading).astype(BF16)
        local_ref[0, :, at] = dot(weights, v)
        path_weight = onpath * jnp.exp(-rate * (length - depth))
        scaled = v.astype(F32) * path_weight
        high = scaled.astype(BF16)
        low = (scaled - high.astype(F32)).astype(BF16)
        update = dot(k, high, ((0,), (0,))) + dot(k, low, ((0,), (0,)))
        update_ref[0, at, :] = update.astype(BF16)


def tree_part(ids, pos, rates, trees, queries, keys, values):
    rows, nodes, width = queries.shape
    heads = width // HD
    token = pl.BlockSpec((1, nodes, width), lambda s, ids, pos: (ids[s], 0, 0))
    return pl.pallas_call(
        functools.partial(tree_kernel, heads),
        out_shape=(
            jax.ShapeDtypeStruct((rows, nodes, width), F32),
            jax.ShapeDtypeStruct((rows, width, HD), BF16),
            jax.ShapeDtypeStruct((rows, nodes, HD), F32),
        ),
        grid_spec=pltpu.PrefetchScalarGridSpec(
            num_scalar_prefetch=2,
            grid=(rows,),
            in_specs=[
                pl.BlockSpec(memory_space=pltpu.SMEM),
                pl.BlockSpec((1, 1, 2 * nodes), lambda s, ids, pos: (pos[s], 0, 0)),
                token,
                token,
                token,
            ],
            out_specs=[
                pl.BlockSpec((1, nodes, width), lambda s, ids, pos: (s, 0, 0)),
                pl.BlockSpec((1, width, HD), lambda s, ids, pos: (s, 0, 0)),
                pl.BlockSpec((1, nodes, HD), lambda s, ids, pos: (s, 0, 0)),
            ],
        ),
        compiler_params=pltpu.CompilerParams(vmem_limit_bytes=24 << 20),
        cost_estimate=pl.CostEstimate(
            flops=rows * heads * 2 * 64 * 128 * 400,
            bytes_accessed=rows * nodes * width * 14,
            transcendentals=rows * heads * 4096,
        ),
        name="tree_part",
    )(ids, pos, rates, trees, queries, keys, values)


def prior_kernel(heads, ids_ref, rates_ref, q_ref, state_ref, local_ref, depth_ref, attn_ref, square_ref):
    depth = depth_ref[0]
    total = jnp.zeros((NODES, HD), F32)
    for h in range(heads):
        at = slice(h * HD, (h + 1) * HD)
        prior = dot(q_ref[0, :, at], state_ref[0, at, :])
        attn = (local_ref[0, :, at] + prior * jnp.exp(-rates_ref[h] * depth)).astype(BF16)
        attn_ref[0, :, at] = attn
        wide = attn.astype(F32)
        total = total + wide * wide
    square_ref[0] = jnp.sum(total.T, axis=0, keepdims=True)


def prior_part(ids, rates, queries, states, local, depth):
    rows, nodes, width = queries.shape
    heads = width // HD
    return pl.pallas_call(
        functools.partial(prior_kernel, heads),
        out_shape=(
            jax.ShapeDtypeStruct((rows, nodes, width), BF16),
            jax.ShapeDtypeStruct((rows, 1, nodes), F32),
        ),
        grid_spec=pltpu.PrefetchScalarGridSpec(
            num_scalar_prefetch=1,
            grid=(rows,),
            in_specs=[
                pl.BlockSpec(memory_space=pltpu.SMEM),
                pl.BlockSpec((1, nodes, width), lambda s, ids: (ids[s], 0, 0)),
                pl.BlockSpec((1, width, HD), lambda s, ids: (s, 0, 0)),
                pl.BlockSpec((1, nodes, width), lambda s, ids: (s, 0, 0)),
                pl.BlockSpec((1, nodes, HD), lambda s, ids: (s, 0, 0)),
            ],
            out_specs=[
                pl.BlockSpec((1, nodes, width), lambda s, ids: (ids[s], 0, 0)),
                pl.BlockSpec((1, 1, nodes), lambda s, ids: (ids[s], 0, 0)),
            ],
        ),
        compiler_params=pltpu.CompilerParams(vmem_limit_bytes=24 << 20),
        cost_estimate=pl.CostEstimate(
            flops=rows * heads * 2 * 64 * 128 * 128,
            bytes_accessed=rows * nodes * width * 12,
            transcendentals=rows * heads * 8192,
        ),
        name="prior_part",
    )(ids, rates, queries, states, local, depth)


def norm_kernel(attn_ref, square_ref, gain_ref, mixed_ref):
    scale = lax.rsqrt(square_ref[0] / (HEADS * HD) + EPS)
    scale = jnp.broadcast_to(scale, (HD, NODES)).T
    width = attn_ref.shape[-1]
    for h in range(width // HD):
        at = slice(h * HD, (h + 1) * HD)
        mixed_ref[0, :, at] = (attn_ref[0, :, at].astype(F32) * scale * gain_ref[:, at]).astype(BF16)


def normalize(attn, square, gain):
    rows, nodes, width = attn.shape
    return pl.pallas_call(
        norm_kernel,
        out_shape=jax.ShapeDtypeStruct(attn.shape, BF16),
        grid=(rows,),
        in_specs=[
            pl.BlockSpec((1, nodes, width), lambda r: (r, 0, 0)),
            pl.BlockSpec((1, 1, nodes), lambda r: (r, 0, 0)),
            pl.BlockSpec((1, width), lambda r: (0, 0)),
        ],
        out_specs=pl.BlockSpec((1, nodes, width), lambda r: (r, 0, 0)),
        cost_estimate=pl.CostEstimate(
            flops=attn.size * 2, bytes_accessed=attn.size * 4, transcendentals=0
        ),
        name="normalize",
    )(attn, square, gain)


def fresh_kernel(
    rows, dest_ref, leading_ref, states_ref, update_ref, out_ref, state, update, fresh, in_sem, up_sem, out_sem
):
    heads = state.shape[1] // HD

    def fetch(j):
        return pltpu.make_async_copy(states_ref.at[j], state.at[j], in_sem.at[j])

    def fetch_update(j):
        return pltpu.make_async_copy(update_ref.at[dest_ref[j]], update.at[j], up_sem.at[j])

    def store(j):
        return pltpu.make_async_copy(fresh.at[j], out_ref.at[j], out_sem.at[j])

    for j in range(rows):
        fetch(j).start()
        fetch_update(j).start()
    for j in range(rows):
        fetch(j).wait()
        fetch_update(j).wait()
        for h in range(heads):
            at = slice(h * HD, (h + 1) * HD)
            fresh[j, at, :] = leading_ref[j, h] * state[j, at, :] + update[j, at, :].astype(F32)
        store(j).start()
    for j in range(rows):
        store(j).wait()


def fresh_states(dest, leading, states, update):
    rows = states.shape[0]
    return pl.pallas_call(
        functools.partial(fresh_kernel, rows),
        out_shape=jax.ShapeDtypeStruct(states.shape, F32),
        in_specs=[
            pl.BlockSpec(memory_space=pltpu.SMEM),
            pl.BlockSpec(memory_space=pltpu.SMEM),
            pl.BlockSpec(memory_space=pl.ANY),
            pl.BlockSpec(memory_space=pl.ANY),
        ],
        out_specs=pl.BlockSpec(memory_space=pl.ANY),
        scratch_shapes=[
            pltpu.VMEM(states.shape, F32),
            pltpu.VMEM(states.shape, BF16),
            pltpu.VMEM(states.shape, F32),
            pltpu.SemaphoreType.DMA((rows,)),
            pltpu.SemaphoreType.DMA((rows,)),
            pltpu.SemaphoreType.DMA((rows,)),
        ],
        compiler_params=pltpu.CompilerParams(vmem_limit_bytes=32 << 20),
        cost_estimate=pl.CostEstimate(
            flops=states.size * 2, bytes_accessed=states.size * 10, transcendentals=0
        ),
        name="fresh_states",
    )(dest, leading, states, update)


def body(queries, keys, values, states, parents, path_nodes, held, rates, gain):
    req_count = lax.axis_size("req")
    req_rank = lax.axis_index("req")
    rows, nodes, width = queries.shape
    heads = width // HD
    flat_states = states.reshape(rows, width, HD)

    table = held.reshape(req_count, rows)
    dest = lax.dynamic_index_in_dim(table, req_rank, 0, keepdims=False) // rows
    hit = table // rows == req_rank
    place = lax.broadcasted_iota(jnp.int32, table.shape, 0) * rows + lax.broadcasted_iota(
        jnp.int32, table.shape, 1
    )
    ids = jnp.sum(jnp.where(hit, table - req_rank * rows, 0), axis=1)
    pos = jnp.sum(jnp.where(hit, place, 0), axis=1)

    trees = lax.all_gather(
        jnp.concatenate([parents, path_nodes], axis=1), "req", axis=0, tiled=True
    )
    sent = cast_states(dest, flat_states)
    arrived = lax.all_to_all(sent, "req", split_axis=0, concat_axis=0, tiled=True)
    local, update, depth = tree_part(
        ids, pos, rates, trees.reshape(req_count * rows, 1, 2 * nodes), queries, keys, values
    )
    update_back = lax.all_to_all(update, "req", split_axis=0, concat_axis=0, tiled=True)
    attn, square = prior_part(ids, rates, queries, arrived, local, depth)
    total = lax.psum(square.reshape(rows, nodes), "head")
    mixed = normalize(attn, total.reshape(rows, 1, nodes), gain.reshape(1, width))

    length = jnp.sum((path_nodes >= 0).astype(F32), axis=1)
    leading = jnp.exp(-rates[None, :] * length[:, None])
    fresh = fresh_states(dest, leading, flat_states, update_back)
    return (mixed, fresh.reshape(rows, heads, HD, HD))


def solution(mesh):
    in_specs = (
        P("req", None, "head"),
        P("req", None, "head"),
        P("req", None, "head"),
        P("req", "head", None, None),
        P("req", None),
        P("req", None),
        P(),
        P("head"),
        P("head"),
    )
    out_specs = (P("req", None, "head"), P("req", "head", None, None))
    return jax.shard_map(body, mesh=mesh, in_specs=in_specs, out_specs=out_specs, check_vma=False)
```

time: 302 us -> 195 us (0.65)
  waiting for transfers between devices: 179 us -> 11.3 us
  blocking collectives: 13.5 us -> 91.5 us
  Pallas kernels: 0 us -> 56.4 us
  matrix products: 31.1 us -> 0 us
  other arithmetic: 21.8 us -> 0.46 us
  local copies, waits for them, and re-layouts: 30.4 us -> 20.1 us
  starting transfers between devices: 23.8 us -> 13.6 us
    all_to_all x4 -> x2, waiting for transfers between devices: 179 us -> 11.3 us  [the longest x1 11.3 us: body(): lax.all_to_all(update, 'req', split_axis=0, concat_axis=0, tiled=True)]
    all_gather x0 -> x1, blocking collectives: none -> 77.5 us  [body(): lax.all_gather(jnp.concatenate([parents, path_nodes], axis=1), 'req', axi...]
    pallas_call x0 -> x5, Pallas kernels: none -> 56.4 us  [the longest x1 27.5 us: tree_part(): pl.pallas_call(functools.partial(tree_kernel, heads), out_shape=(jax.Shap...]
    dot_general x16 -> x0, matrix products: 31.1 us -> none  [the longest x1 10.1 us: attend(): jnp.einsum('rnhd,rnhe->rhde', scaled_keys, v_heads.astype(jnp.float32), p...]
    gather x9 -> x0, local copies, waits for them, and re-layouts: 29.2 us -> none  [the longest x1 8.01 us: body(): new_states = fresh_back[placing]]
    unnamed x15 -> x26, local copies, waits for them, and re-layouts: 0.19 us -> 19.3 us
    add x7 -> x0, other arithmetic: 10.4 us -> none  [the longest x1 10 us: attend(): fresh = leading[:, :, None, None] * states + update]
    all_to_all x4 -> x2, starting transfers between devices: 23.8 us -> 13.6 us  [the longest x1 8.33 us: body(): lax.all_to_all(sent, 'req', split_axis=0, concat_axis=0, tiled=True)]
  transfers between devices with their start and end apart: 4 -> 2, of which waited for: 3 -> 1; matrix products, arithmetic and copies ran while one was open for 20% -> 0% of each run, Pallas kernels for 0% -> 25%
where the time goes in v1:
time: 195 us; the launch traced here: 194 us
  blocking collectives  91.5 us (47%)
  Pallas kernels  56.4 us (29%)
  local copies, waits for them, and re-layouts  20.1 us (10%)
  starting transfers between devices  13.6 us (7%)
  waiting for transfers between devices  11.3 us (6%)
    all_gather x1, blocking collectives, body(): lax.all_gather(jnp.concatenate([parents, path_nodes], axis=1), 'req', axi...  77.5 us
    pallas_call x1, Pallas kernels, tree_part(): pl.pallas_call(functools.partial(tree_kernel, heads), out_shape=(jax.Shap...  27.5 us
    unnamed x26, local copies, waits for them, and re-layouts  19.3 us
    psum x1, blocking collectives, body(): total = lax.psum(square.reshape(rows, nodes), 'head')  14 us
    all_to_all x1, waiting for transfers between devices, body(): lax.all_to_all(update, 'req', split_axis=0, concat_axis=0, tiled=True)  11.3 us
    pallas_call x1, Pallas kernels, prior_part(): pl.pallas_call(functools.partial(prior_kernel, heads), out_shape=(jax.Sha...  11.2 us
    pallas_call x1, Pallas kernels, normalize(): pl.pallas_call(norm_kernel, out_shape=jax.ShapeDtypeStruct(attn.shape, BF...  10.1 us
    all_to_all x1, starting transfers between devices, body(): lax.all_to_all(sent, 'req', split_axis=0, concat_axis=0, tiled=True)  8.33 us
  transfers between devices with their start and end apart: 2, of which 1 were waited for; matrix products, arithmetic and copies ran while one was open for 0% of the time, Pallas kernels for 25%

profile of v1, /device:TPU:0, one launch (start us, length us, event | category | flops | bytes accessed | tf_op | source)
XLA Modules:
  0.0 194.1 jit_solution(11894704171732870996)
XLA Ops:
  0.6 0.8 reshape.28
  1.4 0.0 copy-start
  1.4 3.4 %copy-done = f32[16,8,128,128]{3,2,1,0:T(8,128)S(1)} copy-done((f32[16,8,128,128]{3,2,1,0:T(8,128)S(1)}, f32[16,8,128,128]{3,2,1,0:T(8,128)}, u32[]{:S(2)}) %copy-start) | copy-done | bytes 8388632
  4.8 2.2 %cast_states.1 = bf16[16,1024,128]{2,1,0:T(8,128)(2,1)S(1)} custom-call(s32[16]{0:T(128)S(1)} %and_select_fusion.dest_ref, f32[16,1024,128]{2,1,0:T(8,128)S(1)} %bitcast.12), custom_call_target="tpu_custom_call" | custom-call | bytes 12582912 | tf_op jit(solution)/shard_map/cast_states/pallas_call | solution.py:41
  7.0 0.0 copy-start.2
  7.0 2.0 %copy-done.2 = bf16[16,1024,128]{2,1,0:T(8,128)(2,1)} copy-done((bf16[16,1024,128]{2,1,0:T(8,128)(2,1)}, bf16[16,1024,128]{2,1,0:T(8,128)(2,1)S(1)}, u32[]{:S(2)}) %copy-start.2) | copy-done | bytes 4194328
  9.0 0.0 copy-start.11
  9.0 0.0 copy-start.12
  9.0 0.0 copy-start.3
  9.0 0.0 copy-start.10
  9.0 8.3 %all-to-all-start = ((bf16[16,1024,128]{2,1,0:T(8,128)(2,1)}), bf16[16,1024,128]{2,1,0:T(8,128)(2,1)}, u32[]{:S(2)}, u32[]{:S(2)}) async-start(bf16[16,1024,128]{2,1,0:T(8,128)(2,1)} %copy-done.2), calls=%async_computation | async-start | bytes 8388608 | tf_op jit(solution)/shard_map/all_to_all | solution.py:288
  17.4 0.0 copy-done.11
  17.4 0.0 copy-done.12
  17.4 0.1 pad_add_fusion
  17.5 77.5 %all_gather.3 = s32[256,128]{1,0:T(8,128)S(1)} all-gather(s32[16,128]{1,0:T(8,128)S(1)} %pad_add_fusion), channel_id=1, replica_groups=mesh['req'=16,'head'=8] {'req'}, dimensions={0}, use_global_device_ids=true | all-gather | bytes 139264 | tf_op jit(solution)/shard_map/all_gather | solution.py:284
  95.0 0.2 select_reduce_fusion
  95.1 0.0 copy-done.3
  95.2 0.0 copy-done.10
  95.2 0.0 copy-start.8
  95.2 1.6 copy-done.8
  96.8 0.0 copy-start.9
  96.8 1.6 copy-done.9
  98.4 27.5 %tree_part.1 = (f32[16,64,1024]{2,1,0:T(8,128)S(1)}, bf16[16,1024,128]{2,1,0:T(8,128)(2,1)S(1)}, f32[16,64,128]{2,1,0:T(8,128)S(1)}) custom-call(s32[16]{0:T(128)S(1)} %get-tuple-element.13.ids_ref, s32[16]{0:T(128)S(1)} %get-tuple-element.12.pos_ref, f32[8]{0:T(128)S(1)} %copy-done.10, s32[256,1,128]{2,1,0:T(1,128)S(1)} %bitcast.14, ...), custom_call_target="tpu_custom_call" | custom-call | flops 838860800 | bytes 14680064 | tf_op jit(solution)/shard_map/tree_part/pallas_call | solution.py:104
  125.9 0.0 copy-start.4
  125.9 1.9 copy-done.4
  127.8 0.0 copy-start.5
  127.8 1.9 copy-done.5
  129.7 0.0 all-to-all-done.state_ref
  129.7 5.3 %all-to-all-start.1 = ((bf16[16,1024,128]{2,1,0:T(8,128)(2,1)}), bf16[16,1024,128]{2,1,0:T(8,128)(2,1)}, u32[]{:S(2)}, u32[]{:S(2)}) async-start(bf16[16,1024,128]{2,1,0:T(8,128)(2,1)} %copy-done.4), calls=%async_computation.1 | async-start | bytes 8388608 | tf_op jit(solution)/shard_map/all_to_all | solution.py:292
  135.0 0.1 convert_reduce_fusion
  135.1 0.1 multiply_exponential_fusion.leading_ref
  135.2 0.0 copy-start.6
  135.2 2.2 %copy-done.6 = f32[16,64,1024]{2,1,0:T(8,128)S(1)} copy-done((f32[16,64,1024]{2,1,0:T(8,128)S(1)}, f32[16,64,1024]{2,1,0:T(8,128)}, u32[]{:S(2)}) %copy-start.6) | copy-done | bytes 4194328
  137.4 11.2 %prior_part.1 = (bf16[16,64,1024]{2,1,0:T(8,128)(2,1)S(1)}, f32[16,1,64]{2,1,0:T(1,128)S(1)}) custom-call(s32[16]{0:T(128)S(1)} %get-tuple-element.13.ids_ref, f32[8]{0:T(128)S(1)} %copy-done.10, bf16[16,64,1024]{2,1,0:T(8,128)(2,1)S(1)} %copy-done.3, bf16[16,1024,128]{2,1,0:T(8,128)(2,1)} %all-to-all-done.state_ref, f32[16,64,1024]{2,1,0:T(8,128)S(1)} %copy-done.6, ...), custom_call_target="tpu_custom_call" | custom-call | flops 268435456 | bytes 12582912 | tf_op jit(solution)/shard_map/prior_part/pallas_call | solution.py:153
  148.6 0.0 copy-start.7
  148.6 1.3 copy-done.7
  150.0 14.0 %psum.7.square_ref = f32[16,1,64]{2,1,0:T(1,128)} all-reduce(f32[16,1,64]{2,1,0:T(1,128)S(1)} %get-tuple-element.10), channel_id=1, replica_groups=mesh['req'=16,'head'=8] {'head'}, use_global_device_ids=true, to_apply=%region_2.3 | all-reduce | flops 1024 | bytes 8192 | tf_op jit(solution)/shard_map/psum | solution.py:294
  164.0 10.1 %normalize.1 = bf16[16,64,1024]{2,1,0:T(8,128)(2,1)} custom-call(bf16[16,64,1024]{2,1,0:T(8,128)(2,1)} %copy-done.7, f32[16,1,64]{2,1,0:T(1,128)} %psum.7.square_ref, f32[1,1024]{1,0:T(1,128)} %bitcast.16), custom_call_target="tpu_custom_call" | custom-call | flops 2097152 | bytes 4194304 | tf_op jit(solution)/shard_map/normalize/pallas_call | solution.py:195
  174.1 11.3 %all-to-all-done.1.update_ref = bf16[16,1024,128]{2,1,0:T(8,128)(2,1)} async-done(((bf16[16,1024,128]{2,1,0:T(8,128)(2,1)}), bf16[16,1024,128]{2,1,0:T(8,128)(2,1)}, u32[]{:S(2)}, u32[]{:S(2)}) %all-to-all-start.1) | async-done | bytes 4194336 | tf_op jit(solution)/shard_map/all_to_all | solution.py:292
  185.3 0.0 copy-start.1
  185.3 3.4 %copy-done.1 = f32[16,8,128,128]{3,2,1,0:T(8,128)S(1)} copy-done((f32[16,8,128,128]{3,2,1,0:T(8,128)S(1)}, f32[16,8,128,128]{3,2,1,0:T(8,128)}, u32[]{:S(2)}) %copy-start.1) | copy-done | bytes 8388632
  188.7 5.4 %fresh_states.1 = f32[16,1024,128]{2,1,0:T(8,128)} custom-call(s32[16]{0:T(128)S(1)} %and_select_fusion.dest_ref, f32[16,8]{1,0:T(8,128)S(1)} %multiply_exponential_fusion.leading_ref, f32[16,1024,128]{2,1,0:T(8,128)S(1)} %bitcast.13, bf16[16,1024,128]{2,1,0:T(8,128)(2,1)} %all-to-all-done.1.update_ref), custom_call_target="tpu_custom_call" | custom-call | flops 4194304 | bytes 20971520 | tf_op jit(solution)/shard_map/fresh_states/pallas_call | solution.py:242
  (3 shorter events, 0.0 us)
Async XLA Ops:
  1.4 3.4 %copy-start = (f32[16,8,128,128]{3,2,1,0:T(8,128)S(1)}, f32[16,8,128,128]{3,2,1,0:T(8,128)}, u32[]{:S(2)}) copy-start(f32[16,8,128,128]{3,2,1,0:T(8,128)} %param.12) | copy-start | bytes 25165828
  7.0 2.0 %copy-start.2 = (bf16[16,1024,128]{2,1,0:T(8,128)(2,1)}, bf16[16,1024,128]{2,1,0:T(8,128)(2,1)S(1)}, u32[]{:S(2)}) copy-start(bf16[16,1024,128]{2,1,0:T(8,128)(2,1)S(1)} %cast_states.1) | copy-start | bytes 12582916
  9.0 8.3 %copy-start.11 = (s32[16,64]{1,0:T(8,128)S(1)}, s32[16,64]{1,0:T(8,128)}, u32[]{:S(2)}) copy-start(s32[16,64]{1,0:T(8,128)} %param.14) | copy-start | bytes 12292
  9.0 8.4 %copy-start.12 = (s32[16,64]{1,0:T(8,128)S(1)}, s32[16,64]{1,0:T(8,128)}, u32[]{:S(2)}) copy-start(s32[16,64]{1,0:T(8,128)} %param.13) | copy-start | bytes 12292
  9.0 86.1 %copy-start.3 = (bf16[16,64,1024]{2,1,0:T(8,128)(2,1)S(1)}, bf16[16,64,1024]{2,1,0:T(8,128)(2,1)}, u32[]{:S(2)}) copy-start(bf16[16,64,1024]{2,1,0:T(8,128)(2,1)} %q_ref.3) | copy-start | bytes 6291460
  9.0 86.1 %copy-start.10 = (f32[8]{0:T(128)S(1)}, f32[8]{0:T(128)}, u32[]{:S(2)}) copy-start(f32[8]{0:T(128)} %rates_ref.3) | copy-start | bytes 100
  9.0 120.7 %all-to-all-start = ((bf16[16,1024,128]{2,1,0:T(8,128)(2,1)}), bf16[16,1024,128]{2,1,0:T(8,128)(2,1)}, u32[]{:S(2)}, u32[]{:S(2)}) async-start(bf16[16,1024,128]{2,1,0:T(8,128)(2,1)} %copy-done.2), calls=%async_computation | async-start | bytes 8388608 | tf_op jit(solution)/shard_map/all_to_all | solution.py:288
  95.2 1.6 copy-start.8
  96.8 1.6 copy-start.9
  125.9 1.9 copy-start.4
  127.8 1.9 copy-start.5
  129.7 55.6 %all-to-all-start.1 = ((bf16[16,1024,128]{2,1,0:T(8,128)(2,1)}), bf16[16,1024,128]{2,1,0:T(8,128)(2,1)}, u32[]{:S(2)}, u32[]{:S(2)}) async-start(bf16[16,1024,128]{2,1,0:T(8,128)(2,1)} %copy-done.4), calls=%async_computation.1 | async-start | bytes 8388608 | tf_op jit(solution)/shard_map/all_to_all | solution.py:292
  135.2 2.2 %copy-start.6 = (f32[16,64,1024]{2,1,0:T(8,128)S(1)}, f32[16,64,1024]{2,1,0:T(8,128)}, u32[]{:S(2)}) copy-start(f32[16,64,1024]{2,1,0:T(8,128)} %copy-done.5) | copy-start | bytes 12582916
  148.6 1.3 copy-start.7
  185.3 3.4 %copy-start.1 = (f32[16,8,128,128]{3,2,1,0:T(8,128)S(1)}, f32[16,8,128,128]{3,2,1,0:T(8,128)}, u32[]{:S(2)}) copy-start(f32[16,8,128,128]{3,2,1,0:T(8,128)} %param.12) | copy-start | bytes 25165828

commit v2 on v0

v2 whole, which is shorter than its diff:
```python
import functools

import jax
import jax.numpy as jnp
from jax import lax
from jax.experimental import pallas as pl
from jax.experimental.pallas import tpu as pltpu
from jax.sharding import PartitionSpec as P

HEADS = 64
HD = 128
NODES = 64
EPS = 1e-06
F32 = jnp.float32
BF16 = jnp.bfloat16
TAIL = 16
FAR = 1e30
EARLY = 3
VMEM_LIMIT = 56 << 20
HBM = pl.BlockSpec(memory_space=pltpu.HBM)
SMEM = pl.BlockSpec(memory_space=pltpu.SMEM)
VMEM = pl.BlockSpec(memory_space=pltpu.VMEM)
PARAMS = pltpu.CompilerParams(vmem_limit_bytes=VMEM_LIMIT)


def dot(a, b, dims=((1,), (0,))):
    return lax.dot_general(a, b, (dims, ((), ())), preferred_element_type=F32)


def cost(bytes_accessed, flops=0, transcendentals=0):
    return pl.CostEstimate(
        flops=int(flops), bytes_accessed=int(bytes_accessed), transcendentals=int(transcendentals)
    )


def path_weights(path):
    entry = jnp.broadcast_to(path, (NODES, NODES))
    row = lax.broadcasted_iota(jnp.int32, (NODES, NODES), 0).astype(F32)
    place = lax.broadcasted_iota(jnp.int32, (1, NODES), 1).astype(F32)
    length = jnp.sum((path >= 0.0).astype(F32), axis=1, keepdims=True)
    match = (entry == row).astype(F32)
    onpath = jnp.sum(match, axis=1, keepdims=True)
    age = jnp.sum(match * (length - 1.0 - place), axis=1, keepdims=True)
    return length, jnp.broadcast_to(onpath, (NODES, HD)), jnp.broadcast_to(age, (NODES, HD))


def diagonal(a, b):
    zero = jnp.zeros(a.shape, a.dtype)
    return jnp.concatenate(
        [jnp.concatenate([a, zero], axis=1), jnp.concatenate([zero, b], axis=1)], axis=0
    )


def parts(v, weight):
    scaled = v.astype(F32) * weight
    high = scaled.astype(BF16)
    return high, (scaled - high.astype(F32)).astype(BF16)


def outer(keys, values, weights):
    split = [parts(v, weight) for v, weight in zip(values, weights)]
    if len(keys) == 1:
        both = dot(keys[0], jnp.concatenate(split[0], axis=1), ((0,), (0,)))
        return both[:, :HD] + both[:, HD:]
    stacked = jnp.concatenate(keys + keys, axis=0)
    spread = [diagonal(split[0][at], split[1][at]) for at in (0, 1)]
    return dot(stacked, jnp.concatenate(spread, axis=0), ((0,), (0,)))


def pack_kernel(
    rows, heads, me_ref, held_ref, parents_ref, path_ref, states_ref, keys_ref, values_ref,
    early_ref, late_ref, dest_ref, ids_ref,
    wide, k_all, v_all, early, late, in_sem, out_sem,
):
    height = wide.shape[1]

    def fetch(j):
        return pltpu.make_async_copy(states_ref.at[j], wide.at[j], in_sem.at[3 * j])

    def fetch_pair(j):
        at = ids_ref[dest_ref[j]]
        return (
            pltpu.make_async_copy(keys_ref.at[at], k_all.at[j], in_sem.at[3 * j + 1]),
            pltpu.make_async_copy(values_ref.at[at], v_all.at[j], in_sem.at[3 * j + 2]),
        )

    def store(j):
        return (
            pltpu.make_async_copy(early.at[j], early_ref.at[dest_ref[j]], out_sem.at[2 * j]),
            pltpu.make_async_copy(late.at[j], late_ref.at[dest_ref[j]], out_sem.at[2 * j + 1]),
        )

    for j in range(rows):
        fetch(j).start()
    me = me_ref[0]
    for j in range(rows):
        dest_ref[j] = lax.div(held_ref[me * rows + j], rows)
    for s in range(held_ref.shape[0] // rows):
        found = 0
        for i in range(rows):
            request = held_ref[s * rows + i]
            found = jnp.where(lax.div(request, rows) == me, request - me * rows, found)
        ids_ref[s] = found
    for j in range(rows):
        for copy in fetch_pair(j):
            copy.start()

    def work(j, carry):
        fetch(j).wait()
        for copy in fetch_pair(j):
            copy.wait()
        early[j, :height, :] = wide[j].astype(BF16)
        for h in range(heads):
            at = slice(h * HD, (h + 1) * HD)
            base, ref = (height, early) if h < EARLY else (0, late)
            count = EARLY if h < EARLY else heads - EARLY
            h -= 0 if h < EARLY else EARLY
            ref[j, base + h * NODES : base + (h + 1) * NODES, :] = k_all[j, :, at]
            base += count * NODES
            ref[j, base + h * NODES : base + (h + 1) * NODES, :] = v_all[j, :, at]
        both = jnp.concatenate(
            [parents_ref[pl.ds(j, 1), :], path_ref[pl.ds(j, 1), :]], axis=1
        ).astype(F32)
        early[j, height + 2 * EARLY * NODES :, :] = jnp.broadcast_to(both, (TAIL, HD)).astype(BF16)
        for copy in store(j):
            copy.start()
        return carry

    lax.fori_loop(0, rows, work, 0)
    for j in range(rows):
        for copy in store(j):
            copy.wait()


def pack(me, held, parents, path_nodes, states, keys, values):
    rows, height, width = states.shape
    nodes = keys.shape[1]
    heads = height // HD
    early = (rows, height + 2 * EARLY * nodes + TAIL, width)
    late = (rows, 2 * (heads - EARLY) * nodes, width)
    return pl.pallas_call(
        functools.partial(pack_kernel, rows, heads),
        out_shape=(
            jax.ShapeDtypeStruct(early, BF16),
            jax.ShapeDtypeStruct(late, BF16),
            jax.ShapeDtypeStruct((rows,), jnp.int32),
            jax.ShapeDtypeStruct((held.shape[0] // rows,), jnp.int32),
        ),
        in_specs=[SMEM, SMEM, VMEM, VMEM, HBM, HBM, HBM],
        out_specs=(HBM, HBM, SMEM, SMEM),
        scratch_shapes=[
            pltpu.VMEM(states.shape, F32),
            pltpu.VMEM(keys.shape, BF16),
            pltpu.VMEM(keys.shape, BF16),
            pltpu.VMEM(early, BF16),
            pltpu.VMEM(late, BF16),
            pltpu.SemaphoreType.DMA((3 * rows,)),
            pltpu.SemaphoreType.DMA((2 * rows,)),
        ],
        compiler_params=PARAMS,
        cost_estimate=cost(20e6),
        name="pack",
    )(me, held, parents, path_nodes, states, keys, values)


def gate_kernel(value_ref, after_ref, out_ref):
    pass


def gate(value, after):
    return pl.pallas_call(
        gate_kernel,
        out_shape=jax.ShapeDtypeStruct(value.shape, value.dtype),
        in_specs=[HBM, HBM],
        out_specs=HBM,
        input_output_aliases={0: 0},
        compiler_params=PARAMS,
        cost_estimate=cost(1000),
        name="gate",
    )(value, after)


def attend_kernel(
    rows, heads, ids_ref, rates_ref, early_ref, q_hbm, k_hbm, v_hbm, attn_ref, square_ref,
    q_all, k_all, v_all, state_all, tails, gaps, depths, weights, sem, tail_sem,
):
    tail = early_ref.shape[1] - TAIL
    height = state_all.shape[1]
    tail_copy = pltpu.make_async_copy(early_ref.at[:, pl.ds(tail, TAIL), :], tails, tail_sem)

    def copies(s):
        at = ids_ref[s]
        return (
            pltpu.make_async_copy(q_hbm.at[at], q_all.at[s], sem.at[4 * s]),
            pltpu.make_async_copy(k_hbm.at[at], k_all.at[s], sem.at[4 * s + 1]),
            pltpu.make_async_copy(v_hbm.at[at], v_all.at[s], sem.at[4 * s + 2]),
            pltpu.make_async_copy(
                early_ref.at[s, pl.ds(0, height), :], state_all.at[s], sem.at[4 * s + 3]
            ),
        )

    tail_copy.start()
    for s in range(rows):
        for copy in copies(s):
            copy.start()
    tail_copy.wait()

    row = lax.broadcasted_iota(jnp.int32, (NODES, NODES), 0)
    col = lax.broadcasted_iota(jnp.int32, (NODES, NODES), 1)
    row_wide = row.astype(F32)
    eye = (row == col).astype(F32)
    batch = 4

    def grow(group, carry):
        steps, reaches = [], []
        for b in range(batch):
            parents = tails[group * batch + b].astype(F32)[0:1, :NODES]
            step = (jnp.broadcast_to(parents, (NODES, NODES)) == row_wide).astype(F32)
            steps.append(step.astype(BF16))
            reaches.append(eye + step)
        hops = 2
        while hops < NODES:
            steps = [dot(x, x).astype(BF16) for x in steps]
            reaches = [r + dot(x, r.astype(BF16)) for x, r in zip(steps, reaches)]
            hops *= 2
        for b in range(batch):
            s = group * batch + b
            reach = reaches[b].T
            depth_row = jnp.sum(reaches[b], axis=0, keepdims=True)
            depth = jnp.sum(reach, axis=1, keepdims=True)
            gap = jnp.where(reach > 0.5, depth - depth_row, FAR)
            gaps[s] = jnp.concatenate([gap, gap], axis=1)
            depths[s] = jnp.broadcast_to(depth, (NODES, HD))
        return carry

    lax.fori_loop(0, rows // batch, grow, 0)

    lane = lax.broadcasted_iota(jnp.int32, (1, HD), 1)

    def score(s, carry):
        for copy in copies(s):
            copy.wait()
        gap = gaps[s]
        for pair in range(heads // 2):
            a = slice(2 * pair * HD, (2 * pair + 1) * HD)
            b = slice((2 * pair + 1) * HD, (2 * pair + 2) * HD)
            q = q_all[s, :, 2 * pair * HD : (2 * pair + 2) * HD]
            scores = dot(q, diagonal(k_all[s, :, a], k_all[s, :, b]), ((1,), (1,)))
            rate = jnp.where(lane < NODES, rates_ref[2 * pair], rates_ref[2 * pair + 1])
            weights[s, pair] = (scores * jnp.exp(-rate * gap)).astype(BF16)
        return carry

    def finish(s, carry):
        depth = depths[s]
        at_row = ids_ref[s]
        total = jnp.zeros((NODES, HD), F32)
        for pair in range(heads // 2):
            a = slice(2 * pair * HD, (2 * pair + 1) * HD)
            b = slice((2 * pair + 1) * HD, (2 * pair + 2) * HD)
            q = q_all[s, :, 2 * pair * HD : (2 * pair + 2) * HD]
            local = dot(weights[s, pair], diagonal(v_all[s, :, a], v_all[s, :, b]))
            prior = dot(q, diagonal(state_all[s, a, :], state_all[s, b, :]))
            for h, at, cut in ((2 * pair, a, slice(0, HD)), (2 * pair + 1, b, slice(HD, 2 * HD))):
                decay = jnp.exp(-rates_ref[h] * depth)
                attn = (local[:, cut] + prior[:, cut] * decay).astype(BF16)
                attn_ref[at_row, :, at] = attn
                wide = attn.astype(F32)
                total = total + wide * wide
        square_ref[pl.ds(at_row, 1), :] = jnp.sum(total.T, axis=0, keepdims=True)
        return carry

    lax.fori_loop(0, rows, score, 0)
    lax.fori_loop(0, rows, finish, 0, unroll=2)


def attend(ids, rates, early, queries, keys, values):
    rows, nodes, width = queries.shape
    return pl.pallas_call(
        functools.partial(attend_kernel, rows, width // HD),
        out_shape=(
            jax.ShapeDtypeStruct((rows, nodes, width), BF16),
            jax.ShapeDtypeStruct((rows, nodes), F32),
        ),
        in_specs=[SMEM, SMEM, HBM, HBM, HBM, HBM],
        out_specs=(VMEM, VMEM),
        scratch_shapes=[
            pltpu.VMEM((rows, nodes, width), BF16),
            pltpu.VMEM((rows, nodes, width), BF16),
            pltpu.VMEM((rows, nodes, width), BF16),
            pltpu.VMEM((rows, width, HD), BF16),
            pltpu.VMEM((rows, TAIL, HD), BF16),
            pltpu.VMEM((rows, nodes, 2 * nodes), F32),
            pltpu.VMEM((rows, nodes, HD), F32),
            pltpu.VMEM((rows, width // HD // 2, nodes, 2 * nodes), BF16),
            pltpu.SemaphoreType.DMA((4 * rows,)),
            pltpu.SemaphoreType.DMA,
        ],
        compiler_params=PARAMS,
        cost_estimate=cost(50e6, 1e9),
        name="attend",
    )(ids, rates, early, queries, keys, values)


def update_kernel(
    rows, first, heads, base, dest_ref, rates_ref, path_ref, states_ref, pairs_ref, *refs
):
    out_ref, state, fresh, pair, onpaths, ages, lengths, in_sem, pair_sem, out_sem = refs[-10:]
    direct = pair.shape[0] == 1
    part = pl.ds(first * HD, heads * HD)

    def fetch(j):
        copies = [pltpu.make_async_copy(states_ref.at[j, part, :], state.at[j], in_sem.at[j])]
        if not direct:
            source = pairs_ref.at[dest_ref[j], pl.ds(base, 2 * heads * NODES), :]
            copies.append(pltpu.make_async_copy(source, pair.at[j], pair_sem.at[j]))
        return copies

    def store(j):
        return pltpu.make_async_copy(fresh.at[j], out_ref.at[j, part, :], out_sem.at[j])

    for j in range(rows):
        for copy in fetch(j):
            copy.start()

    for j in range(rows):
        length, onpath, age = path_weights(path_ref[j : j + 1, :].astype(F32))
        onpaths[j], ages[j] = onpath, age
        lengths[j] = jnp.broadcast_to(length, (8, HD))

    def work(j, carry):
        onpath, age, length = onpaths[j], ages[j], lengths[j, 0:1, :]
        for copy in fetch(j):
            copy.wait()
        ready, row = (pairs_ref, dest_ref[j]) if direct else (pair, j)
        for start in range(0, heads, 2):
            group = range(start, min(start + 2, heads))
            update = outer(
                [ready[row, h * NODES : (h + 1) * NODES, :] for h in group],
                [ready[row, (heads + h) * NODES : (heads + h + 1) * NODES, :] for h in group],
                [onpath * jnp.exp(-rates_ref[first + h] * age) for h in group],
            )
            for n, h in enumerate(group):
                at = slice(h * HD, (h + 1) * HD)
                kept = jnp.exp(-rates_ref[first + h] * length) * state[j, at, :]
                fresh[j, at, :] = kept + update[:, n * HD : (n + 1) * HD]
        store(j).start()
        return carry

    lax.fori_loop(0, rows, work, 0, unroll=2)
    for j in range(rows):
        store(j).wait()


def update_states(first, heads, base, dest, rates, path_nodes, states, pairs, partial):
    rows, _, width = states.shape
    earlier = [] if partial is None else [partial]
    direct = pairs.shape[1] == 2 * heads * NODES
    return pl.pallas_call(
        functools.partial(update_kernel, rows, first, heads, base),
        out_shape=jax.ShapeDtypeStruct(states.shape, F32),
        in_specs=[SMEM, SMEM, VMEM, HBM, VMEM if direct else HBM] + [HBM] * len(earlier),
        out_specs=HBM,
        input_output_aliases={5: 0} if earlier else {},
        scratch_shapes=[
            pltpu.VMEM((rows, heads * HD, width), F32),
            pltpu.VMEM((rows, heads * HD, width), F32),
            pltpu.VMEM((1 if direct else rows, 2 * heads * NODES, HD), BF16),
            pltpu.VMEM((rows, NODES, HD), F32),
            pltpu.VMEM((rows, NODES, HD), F32),
            pltpu.VMEM((rows, 8, HD), F32),
            pltpu.SemaphoreType.DMA((rows,)),
            pltpu.SemaphoreType.DMA((rows,)),
            pltpu.SemaphoreType.DMA((rows,)),
        ],
        compiler_params=pltpu.CompilerParams(vmem_limit_bytes=(49 if direct else 56) << 20),
        cost_estimate=cost(10e6, 5e8),
        name="update_states",
    )(dest, rates, path_nodes, states, pairs, *earlier)


def body(queries, keys, values, states, parents, path_nodes, held, rates, gain):
    me = lax.axis_index("req")
    rows, nodes, width = queries.shape
    heads = width // HD
    flat_states = states.reshape(rows, width, HD)

    def swap(x):
        return lax.all_to_all(x, "req", split_axis=0, concat_axis=0, tiled=True)

    early, late, dest, ids = pack(
        me.reshape(1), held, parents, path_nodes, flat_states, keys, values
    )
    early = swap(early)
    late = swap(gate(late, early))
    attn, square = attend(ids, rates, early, queries, keys, values)
    fresh = update_states(0, EARLY, width, dest, rates, path_nodes, flat_states, early, None)
    head_count = lax.axis_size("head")
    square = square + lax.ppermute(square, "head", [(i, i ^ 1) for i in range(head_count)])
    others = [
        lax.ppermute(square, "head", [(i, (i + step) % head_count) for i in range(head_count)])
        for step in range(2, head_count, 2)
    ]
    square = square + sum(others)
    scaling = lax.rsqrt(square / (HEADS * HD) + EPS)
    mixed = (attn.astype(F32) * scaling[:, :, None] * gain).astype(BF16)
    fresh = update_states(
        EARLY, heads - EARLY, 0, dest, rates, path_nodes, flat_states, late, fresh
    )
    return (mixed, fresh.reshape(rows, heads, HD, HD))


def solution(mesh):
    in_specs = (
        P("req", None, "head"),
        P("req", None, "head"),
        P("req", None, "head"),
        P("req", "head", None, None),
        P("req", None),
        P("req", None),
        P(),
        P("head"),
        P("head"),
    )
    out_specs = (P("req", None, "head"), P("req", "head", None, None))
    return jax.shard_map(body, mesh=mesh, in_specs=in_specs, out_specs=out_specs, check_vma=False)
```

time: 302 us -> 134 us (0.44)
  waiting for transfers between devices: 179 us -> 4.29 us
  blocking collectives: 13.5 us -> 76.7 us
  Pallas kernels: 0 us -> 40.8 us
  matrix products: 31.1 us -> 0 us
  local copies, waits for them, and re-layouts: 30.4 us -> 0.02 us
  other arithmetic: 21.8 us -> 2.57 us
  starting transfers between devices: 23.8 us -> 8.26 us
    all_to_all x4 -> x1, waiting for transfers between devices: 179 us -> 2.92 us  [swap(): return lax.all_to_all(x, 'req', split_axis=0, concat_axis=0, tiled=True)]
    all_to_all x0 -> x1, blocking collectives: none -> 76.7 us  [swap(): return lax.all_to_all(x, 'req', split_axis=0, concat_axis=0, tiled=True)]
    pallas_call x0 -> x5, Pallas kernels: none -> 40.8 us  [the longest x1 18.5 us: attend(): pl.pallas_call(functools.partial(attend_kernel, rows, width // HD), out_s...]
    dot_general x16 -> x0, matrix products: 31.1 us -> none  [the longest x1 10.1 us: attend(): jnp.einsum('rnhd,rnhe->rhde', scaled_keys, v_heads.astype(jnp.float32), p...]
    gather x9 -> x0, local copies, waits for them, and re-layouts: 29.2 us -> none  [the longest x1 8.01 us: body(): new_states = fresh_back[placing]]
    all_to_all x4 -> x1, starting transfers between devices: 23.8 us -> 3.73 us  [swap(): return lax.all_to_all(x, 'req', split_axis=0, concat_axis=0, tiled=True)]
    psum x1 -> x0, blocking collectives: 13.5 us -> none  [body(): total = lax.psum(partial_value, 'head')]
    add x7 -> x1, other arithmetic: 10.4 us -> 0.7 us  [body(): square + lax.ppermute(square, 'head', [(i, i ^ 1) for i in range(head_cou...]
  transfers between devices with their start and end apart: 4 -> 5, of which waited for: 3 -> 2; matrix products, arithmetic and copies ran while one was open for 20% -> 2% of each run, Pallas kernels for 0% -> 19%
where the time goes in v2:
time: 134 us; the launch traced here: 133 us
  blocking collectives  76.7 us (57%)
  Pallas kernels  40.8 us (30%)
  starting transfers between devices  8.26 us (6%)
  waiting for transfers between devices  4.29 us (3%)
  other arithmetic  2.57 us (2%)
    all_to_all x1, blocking collectives, swap(): return lax.all_to_all(x, 'req', split_axis=0, concat_axis=0, tiled=True)  76.7 us
    pallas_call x1, Pallas kernels, attend(): pl.pallas_call(functools.partial(attend_kernel, rows, width // HD), out_s...  18.5 us
    pallas_call x2, Pallas kernels, update_states(): pl.pallas_call(functools.partial(update_kernel, rows, first, heads, base)...  13.3 us
    pallas_call x1, Pallas kernels, pack(): pl.pallas_call(functools.partial(pack_kernel, rows, heads), out_shape=(ja...  8.95 us
    ppermute x3, starting transfers between devices, body(): lax.ppermute(square, 'head', [(i, (i + step) % head_count) for i in range...  4.44 us
    all_to_all x1, starting transfers between devices, swap(): return lax.all_to_all(x, 'req', split_axis=0, concat_axis=0, tiled=True)  3.73 us
    all_to_all x1, waiting for transfers between devices, swap(): return lax.all_to_all(x, 'req', split_axis=0, concat_axis=0, tiled=True)  2.92 us
  transfers between devices with their start and end apart: 5, of which 2 were waited for; matrix products, arithmetic and copies ran while one was open for 2% of the time, Pallas kernels for 19%

profile of v2, /device:TPU:0, one launch (start us, length us, event | category | flops | bytes accessed | tf_op | source)
XLA Modules:
  0.0 133.4 jit_solution(16549806472125179766)
XLA Ops:
  0.6 9.0 %pack.1 = (bf16[16,1424,128]{2,1,0:T(8,128)(2,1)}, bf16[16,640,128]{2,1,0:T(8,128)(2,1)}, s32[16]{0:T(128)}, s32[16]{0:T(128)}) custom-call(s32[1]{0:T(128)} %bitcast.me_ref, s32[256]{0:T(256)} %held_ref.1, s32[16,64]{1,0:T(8,128)} %parents_ref.1, s32[16,64]{1,0:T(8,128)} %path_ref.5, f32[16,1024,128]{2,1,0:T(8,128)} %bitcast.3, ...), custom_call_target="tpu_custom_call" | custom-call | bytes 20000000 | tf_op jit(solution)/shard_map/pack/pallas_call | solution.py:141
  9.6 76.7 %all_to_all.10.early_ref.after_ref.pairs_ref = bf16[16,1424,128]{2,1,0:T(8,128)(2,1)} all-to-all(bf16[16,1424,128]{2,1,0:T(8,128)(2,1)} %get-tuple-element.9), channel_id=1, replica_groups=mesh['req'=16,'head'=8] {'req'}, dimensions={0} | all-to-all | bytes 11665408 | tf_op jit(solution)/shard_map/all_to_all | solution.py:388
  86.3 3.7 %all-to-all-start.1 = ((bf16[16,640,128]{2,1,0:T(8,128)(2,1)}), bf16[16,640,128]{2,1,0:T(8,128)(2,1)S(1)}, u32[]{:S(2)}, u32[]{:S(2)}) async-start(bf16[16,640,128]{2,1,0:T(8,128)(2,1)} %gate.1), calls=%async_computation.1 | async-start | bytes 5242880 | tf_op jit(solution)/shard_map/all_to_all | solution.py:388
  90.0 18.5 %attend.1 = (bf16[16,64,1024]{2,1,0:T(8,128)(2,1)}, f32[16,64]{1,0:T(8,128)}) custom-call(s32[16]{0:T(128)} %get-tuple-element.8.ids_ref, f32[8]{0:T(128)} %rates_ref.5, bf16[16,1424,128]{2,1,0:T(8,128)(2,1)} %all_to_all.10.early_ref.after_ref.pairs_ref, bf16[16,64,1024]{2,1,0:T(8,128)(2,1)} %q_hbm.1, bf16[16,64,1024]{2,1,0:T(8,128)(2,1)} %k_hbm.1, ...), custom_call_target="tpu_custom_call" | custom-call | flops 1000000000 | bytes 50000000 | tf_op jit(solution)/shard_map/attend/pallas_call | solution.py:278
  108.6 0.1 collective-permute-start
  108.7 1.4 %collective-permute-done = f32[16,64]{1,0:T(8,128)S(1)} collective-permute-done((f32[16,64]{1,0:T(8,128)}, f32[16,64]{1,0:T(8,128)S(1)}, u32[]{:S(2)}, u32[]{:S(2)}) %collective-permute-start) | collective-permute-done | bytes 4128 | tf_op jit(solution)/shard_map/ppermute | solution.py:398
  110.0 0.7 add.18
  110.7 2.8 %collective-permute-start.3 = (f32[16,64]{1,0:T(8,128)S(1)}, f32[16,64]{1,0:T(8,128)S(1)}, u32[]{:S(2)}, u32[]{:S(2)}) collective-permute-start(f32[16,64]{1,0:T(8,128)S(1)} %add.18), channel_id=1, source_target_pairs={{0,6},{1,7},{2,0},{3,1},{4,2},{5,3},{6,4},{7,5},{8,14},{9,15},{10,... | collective-permute-start | bytes 12296 | tf_op jit(solution)/shard_map/ppermute | solution.py:400
  113.5 0.8 collective-permute-start.2
  114.3 0.9 collective-permute-start.1
  115.2 0.0 copy-start.3
  115.2 0.0 copy-start.4
  115.2 6.6 %update_states.2.refs_0_ = f32[16,1024,128]{2,1,0:T(8,128)} custom-call(s32[16]{0:T(128)} %get-tuple-element.12.dest_ref, f32[8]{0:T(128)} %rates_ref.5, s32[16,64]{1,0:T(8,128)} %path_ref.5, f32[16,1024,128]{2,1,0:T(8,128)} %bitcast.4, bf16[16,1424,128]{2,1,0:T(8,128)(2,1)} %all_to_all.10.early_ref.after_ref.pairs_ref), custom_call_target="tpu_custom_call" | custom-call | flops 500000000 | bytes 10000000 | tf_op jit(solution)/shard_map/update_states/pallas_call | solution.py:358
  121.8 0.0 copy-start
  121.8 0.0 copy-start.1
  121.8 0.0 copy-start.2
  121.8 0.0 collective-permute-done.3
  121.8 0.0 collective-permute-done.2
  121.8 0.0 collective-permute-done.1
  121.8 0.0 copy-done.3
  121.9 0.0 copy-done.4
  121.9 1.9 %multiply_convert_fusion = bf16[16,64,1024]{2,1,0:T(8,128)(2,1)} fusion(bf16[16,64,1024]{2,1,0:T(8,128)(2,1)S(1)} %copy-done.3, f32[1024]{0:T(1024)S(1)} %copy-done.4, f32[16,64]{1,0:T(8,128)S(1)} %add_rsqrt_fusion), kind=kLoop, calls=%fused_computation | loop fusion | flops 4194304 | bytes 4202496 | tf_op jit(solution)/shard_map/convert_element_type | solution.py:405
  123.7 2.9 %all-to-all-done.1.pairs_ref = bf16[16,640,128]{2,1,0:T(8,128)(2,1)S(1)} async-done(((bf16[16,640,128]{2,1,0:T(8,128)(2,1)}), bf16[16,640,128]{2,1,0:T(8,128)(2,1)S(1)}, u32[]{:S(2)}, u32[]{:S(2)}) %all-to-all-start.1) | async-done | bytes 2621472 | tf_op jit(solution)/shard_map/all_to_all | solution.py:388
  126.6 0.0 copy-done
  126.7 0.0 copy-done.1
  126.7 0.0 copy-done.2
  126.7 6.7 %update_states.3 = f32[16,1024,128]{2,1,0:T(8,128)} custom-call(s32[16]{0:T(128)S(1)} %copy-done.2, f32[8]{0:T(128)S(1)} %copy-done.1, s32[16,64]{1,0:T(8,128)S(1)} %copy-done, f32[16,1024,128]{2,1,0:T(8,128)} %bitcast.5, bf16[16,640,128]{2,1,0:T(8,128)(2,1)S(1)} %all-to-all-done.1.pairs_ref, ...), custom_call_target="tpu_custom_call", output_to_operand_aliasing={{}: (5, {})} | custom-call | flops 500000000 | bytes 10000000 | tf_op jit(solution)/shard_map/update_states/pallas_call | solution.py:358
  (2 shorter events, 0.0 us)
Async XLA Ops:
  86.3 40.4 %all-to-all-start.1 = ((bf16[16,640,128]{2,1,0:T(8,128)(2,1)}), bf16[16,640,128]{2,1,0:T(8,128)(2,1)S(1)}, u32[]{:S(2)}, u32[]{:S(2)}) async-start(bf16[16,640,128]{2,1,0:T(8,128)(2,1)} %gate.1), calls=%async_computation.1 | async-start | bytes 5242880 | tf_op jit(solution)/shard_map/all_to_all | solution.py:388
  108.6 1.5 %collective-permute-start = (f32[16,64]{1,0:T(8,128)}, f32[16,64]{1,0:T(8,128)S(1)}, u32[]{:S(2)}, u32[]{:S(2)}) collective-permute-start(f32[16,64]{1,0:T(8,128)} %get-tuple-element.11), channel_id=1, source_target_pairs={{0,1},{1,0},{2,3},{3,2},{4,5},{5,4},{6,7},{7,6},{8,9},{9,8},{10,11... | collective-permute-start | bytes 12296 | tf_op jit(solution)/shard_map/ppermute | solution.py:398
  110.7 11.1 %collective-permute-start.3 = (f32[16,64]{1,0:T(8,128)S(1)}, f32[16,64]{1,0:T(8,128)S(1)}, u32[]{:S(2)}, u32[]{:S(2)}) collective-permute-start(f32[16,64]{1,0:T(8,128)S(1)} %add.18), channel_id=1, source_target_pairs={{0,6},{1,7},{2,0},{3,1},{4,2},{5,3},{6,4},{7,5},{8,14},{9,15},{10,... | collective-permute-start | bytes 12296 | tf_op jit(solution)/shard_map/ppermute | solution.py:400
  113.5 8.3 %collective-permute-start.2 = (f32[16,64]{1,0:T(8,128)S(1)}, f32[16,64]{1,0:T(8,128)S(1)}, u32[]{:S(2)}, u32[]{:S(2)}) collective-permute-start(f32[16,64]{1,0:T(8,128)S(1)} %add.18), channel_id=1, source_target_pairs={{0,4},{1,5},{2,6},{3,7},{4,0},{5,1},{6,2},{7,3},{8,12},{9,13},{10,... | collective-permute-start | bytes 12296 | tf_op jit(solution)/shard_map/ppermute | solution.py:400
  114.3 7.5 %collective-permute-start.1 = (f32[16,64]{1,0:T(8,128)S(1)}, f32[16,64]{1,0:T(8,128)S(1)}, u32[]{:S(2)}, u32[]{:S(2)}) collective-permute-start(f32[16,64]{1,0:T(8,128)S(1)} %add.18), channel_id=1, source_target_pairs={{0,2},{1,3},{2,4},{3,5},{4,6},{5,7},{6,0},{7,1},{8,10},{9,11},{10,... | collective-permute-start | bytes 12296 | tf_op jit(solution)/shard_map/ppermute | solution.py:400
  115.2 6.7 %copy-start.3 = (bf16[16,64,1024]{2,1,0:T(8,128)(2,1)S(1)}, bf16[16,64,1024]{2,1,0:T(8,128)(2,1)}, u32[]{:S(2)}) copy-start(bf16[16,64,1024]{2,1,0:T(8,128)(2,1)} %get-tuple-element.10) | copy-start | bytes 6291460
  115.2 6.7 %copy-start.4 = (f32[1024]{0:T(1024)S(1)}, f32[1024]{0:T(1024)}, u32[]{:S(2)}) copy-start(f32[1024]{0:T(1024)} %param.17) | copy-start | bytes 12292
  121.8 4.9 %copy-start = (s32[16,64]{1,0:T(8,128)S(1)}, s32[16,64]{1,0:T(8,128)}, u32[]{:S(2)}) copy-start(s32[16,64]{1,0:T(8,128)} %path_ref.5) | copy-start | bytes 12292
  121.8 4.9 %copy-start.1 = (f32[8]{0:T(128)S(1)}, f32[8]{0:T(128)}, u32[]{:S(2)}) copy-start(f32[8]{0:T(128)} %rates_ref.5) | copy-start | bytes 100
  121.8 4.9 %copy-start.2 = (s32[16]{0:T(128)S(1)}, s32[16]{0:T(128)}, u32[]{:S(2)}) copy-start(s32[16]{0:T(128)} %get-tuple-element.12.dest_ref) | copy-start | bytes 196

commit v3 on v2

--- a/solution.py
+++ b/solution.py
@@ -15,7 +15,7 @@
 BF16 = jnp.bfloat16
 TAIL = 16
 FAR = 1e30
-EARLY = 3
+EARLY = 4
 VMEM_LIMIT = 56 << 20
 HBM = pl.BlockSpec(memory_space=pltpu.HBM)
 SMEM = pl.BlockSpec(memory_space=pltpu.SMEM)
@@ -33,15 +33,13 @@
     )
 
 
-def path_weights(path):
-    entry = jnp.broadcast_to(path, (NODES, NODES))
-    row = lax.broadcasted_iota(jnp.int32, (NODES, NODES), 0).astype(F32)
-    place = lax.broadcasted_iota(jnp.int32, (1, NODES), 1).astype(F32)
-    length = jnp.sum((path >= 0.0).astype(F32), axis=1, keepdims=True)
-    match = (entry == row).astype(F32)
-    onpath = jnp.sum(match, axis=1, keepdims=True)
-    age = jnp.sum(match * (length - 1.0 - place), axis=1, keepdims=True)
-    return length, jnp.broadcast_to(onpath, (NODES, HD)), jnp.broadcast_to(age, (NODES, HD))
+def path_weights(path, length):
+    row = lax.broadcasted_iota(jnp.int32, (NODES, NODES), 0)
+    match = (jnp.broadcast_to(path, (NODES, NODES)) == row).astype(F32).astype(BF16)
+    place = lax.broadcasted_iota(jnp.int32, (NODES, HD), 0).astype(F32)
+    ages = jnp.maximum(length - 1.0 - place, 0.0).astype(BF16)
+    both = dot(match, jnp.concatenate([jnp.ones((NODES, HD), BF16), ages], axis=1))
+    return both[:, :HD], both[:, HD:]
 
 
 def diagonal(a, b):
@@ -68,9 +66,9 @@
 
 
 def pack_kernel(
-    rows, heads, me_ref, held_ref, parents_ref, path_ref, states_ref, keys_ref, values_ref,
-    early_ref, late_ref, dest_ref, ids_ref,
-    wide, k_all, v_all, early, late, in_sem, out_sem,
+    rows, heads, me_ref, held_hbm, parents_hbm, path_hbm, states_ref, keys_ref, values_ref,
+    early_ref, late_ref, dest_hbm, ids_hbm,
+    wide, k_all, v_all, early, late, held_ref, parents_ref, path_ref, dest_ref, ids_ref, in_sem, out_sem, small_sem,
 ):
     height = wide.shape[1]
 
@@ -90,8 +88,21 @@
             pltpu.make_async_copy(late.at[j], late_ref.at[dest_ref[j]], out_sem.at[2 * j + 1]),
         )
 
+    held_copy = pltpu.make_async_copy(held_hbm, held_ref, small_sem.at[0])
+    tree_copies = (
+        pltpu.make_async_copy(parents_hbm, parents_ref, small_sem.at[1]),
+        pltpu.make_async_copy(path_hbm, path_ref, small_sem.at[2]),
+    )
+    index_copies = (
+        pltpu.make_async_copy(dest_ref, dest_hbm, small_sem.at[3]),
+        pltpu.make_async_copy(ids_ref, ids_hbm, small_sem.at[4]),
+    )
+    held_copy.start()
+    for copy in tree_copies:
+        copy.start()
     for j in range(rows):
         fetch(j).start()
+    held_copy.wait()
     me = me_ref[0]
     for j in range(rows):
         dest_ref[j] = lax.div(held_ref[me * rows + j], rows)
@@ -104,6 +115,10 @@
     for j in range(rows):
         for copy in fetch_pair(j):
             copy.start()
+    for copy in index_copies:
+        copy.start()
+    for copy in tree_copies:
+        copy.wait()
 
     def work(j, carry):
         fetch(j).wait()
@@ -127,6 +142,8 @@
         return carry
 
     lax.fori_loop(0, rows, work, 0)
+    for copy in index_copies:
+        copy.wait()
     for j in range(rows):
         for copy in store(j):
             copy.wait()
@@ -146,16 +163,22 @@
             jax.ShapeDtypeStruct((rows,), jnp.int32),
             jax.ShapeDtypeStruct((held.shape[0] // rows,), jnp.int32),
         ),
-        in_specs=[SMEM, SMEM, VMEM, VMEM, HBM, HBM, HBM],
-        out_specs=(HBM, HBM, SMEM, SMEM),
+        in_specs=[SMEM, HBM, HBM, HBM, HBM, HBM, HBM],
+        out_specs=(HBM, HBM, HBM, HBM),
         scratch_shapes=[
             pltpu.VMEM(states.shape, F32),
             pltpu.VMEM(keys.shape, BF16),
             pltpu.VMEM(keys.shape, BF16),
             pltpu.VMEM(early, BF16),
             pltpu.VMEM(late, BF16),
+            pltpu.SMEM(held.shape, jnp.int32),
+            pltpu.VMEM(parents.shape, jnp.int32),
+            pltpu.VMEM(path_nodes.shape, jnp.int32),
+            pltpu.SMEM((rows,), jnp.int32),
+            pltpu.SMEM((held.shape[0] // rows,), jnp.int32),
             pltpu.SemaphoreType.DMA((3 * rows,)),
             pltpu.SemaphoreType.DMA((2 * rows,)),
+            pltpu.SemaphoreType.DMA((5,)),
         ],
         compiler_params=PARAMS,
         cost_estimate=cost(20e6),
@@ -181,8 +204,8 @@
 
 
 def attend_kernel(
-    rows, heads, ids_ref, rates_ref, early_ref, q_hbm, k_hbm, v_hbm, attn_ref, square_ref,
-    q_all, k_all, v_all, state_all, tails, gaps, depths, weights, sem, tail_sem,
+    rows, heads, ids_hbm, rates_hbm, early_ref, q_hbm, k_hbm, v_hbm, attn_ref, square_ref,
+    q_all, k_all, v_all, state_all, tails, gaps, depths, weights, ids_ref, rates_ref, sem, tail_sem, small_sem,
 ):
     tail = early_ref.shape[1] - TAIL
     height = state_all.shape[1]
@@ -199,10 +222,16 @@
             ),
         )
 
+    ids_copy = pltpu.make_async_copy(ids_hbm, ids_ref, small_sem.at[0])
+    rates_copy = pltpu.make_async_copy(rates_hbm, rates_ref, small_sem.at[1])
+    ids_copy.start()
+    rates_copy.start()
     tail_copy.start()
+    ids_copy.wait()
     for s in range(rows):
         for copy in copies(s):
             copy.start()
+    rates_copy.wait()
     tail_copy.wait()
 
     row = lax.broadcasted_iota(jnp.int32, (NODES, NODES), 0)
@@ -269,7 +298,7 @@
         square_ref[pl.ds(at_row, 1), :] = jnp.sum(total.T, axis=0, keepdims=True)
         return carry
 
-    lax.fori_loop(0, rows, score, 0)
+    lax.fori_loop(0, rows, score, 0, unroll=2)
     lax.fori_loop(0, rows, finish, 0, unroll=2)
 
 
@@ -281,7 +310,7 @@
             jax.ShapeDtypeStruct((rows, nodes, width), BF16),
             jax.ShapeDtypeStruct((rows, nodes), F32),
         ),
-        in_specs=[SMEM, SMEM, HBM, HBM, HBM, HBM],
+        in_specs=[HBM, HBM, HBM, HBM, HBM, HBM],
         out_specs=(VMEM, VMEM),
         scratch_shapes=[
             pltpu.VMEM((rows, nodes, width), BF16),
@@ -292,8 +321,11 @@
             pltpu.VMEM((rows, nodes, 2 * nodes), F32),
             pltpu.VMEM((rows, nodes, HD), F32),
             pltpu.VMEM((rows, width // HD // 2, nodes, 2 * nodes), BF16),
+            pltpu.SMEM(ids.shape, jnp.int32),
+            pltpu.SMEM(rates.shape, F32),
             pltpu.SemaphoreType.DMA((4 * rows,)),
             pltpu.SemaphoreType.DMA,
+            pltpu.SemaphoreType.DMA((2,)),
         ],
         compiler_params=PARAMS,
         cost_estimate=cost(50e6, 1e9),
@@ -302,9 +334,10 @@
 
 
 def update_kernel(
-    rows, first, heads, base, dest_ref, rates_ref, path_ref, states_ref, pairs_ref, *refs
+    rows, first, heads, base, dest_hbm, rates_hbm, path_hbm, states_ref, pairs_ref, *refs
 ):
-    out_ref, state, fresh, pair, onpaths, ages, lengths, in_sem, pair_sem, out_sem = refs[-10:]
+    out_ref, state, fresh, pair, onpaths, ages, lengths = refs[-14:-7]
+    dest_ref, rates_ref, path_ref, in_sem, pair_sem, out_sem, small_sem = refs[-7:]
     direct = pair.shape[0] == 1
     part = pl.ds(first * HD, heads * HD)
 
@@ -318,14 +351,32 @@
     def store(j):
         return pltpu.make_async_copy(fresh.at[j], out_ref.at[j, part, :], out_sem.at[j])
 
-    for j in range(rows):
+    small = [
+        pltpu.make_async_copy(source, target, small_sem.at[n])
+        for n, (source, target) in enumerate(
+            ((dest_hbm, dest_ref), (path_hbm, path_ref), (rates_hbm, rates_ref))
+        )
+    ]
+    for copy in small:
+        copy.start()
+    ahead = rows if direct else rows // 2
+    if not direct:
+        small[0].wait()
+    for j in range(ahead):
         for copy in fetch(j):
             copy.start()
-
-    for j in range(rows):
-        length, onpath, age = path_weights(path_ref[j : j + 1, :].astype(F32))
-        onpaths[j], ages[j] = onpath, age
+    for copy in small[0 if direct else 1 :]:
+        copy.wait()
+
+    counts = jnp.sum((path_ref[...] >= 0).astype(F32), axis=1, keepdims=True)
+    counts = jnp.broadcast_to(counts, (rows, HD))
+    for j in range(rows):
+        length = counts[j : j + 1, :]
+        onpaths[j], ages[j] = path_weights(path_ref[j : j + 1, :], length)
         lengths[j] = jnp.broadcast_to(length, (8, HD))
+    for j in range(ahead, rows):
+        for copy in fetch(j):
+            copy.start()
 
     def work(j, carry):
         onpath, age, length = onpaths[j], ages[j], lengths[j, 0:1, :]
@@ -358,7 +409,7 @@
     return pl.pallas_call(
         functools.partial(update_kernel, rows, first, heads, base),
         out_shape=jax.ShapeDtypeStruct(states.shape, F32),
-        in_specs=[SMEM, SMEM, VMEM, HBM, VMEM if direct else HBM] + [HBM] * len(earlier),
+        in_specs=[HBM, HBM, HBM, HBM, VMEM if direct else HBM] + [HBM] * len(earlier),
         out_specs=HBM,
         input_output_aliases={5: 0} if earlier else {},
         scratch_shapes=[
@@ -368,9 +419,13 @@
             pltpu.VMEM((rows, NODES, HD), F32),
             pltpu.VMEM((rows, NODES, HD), F32),
             pltpu.VMEM((rows, 8, HD), F32),
+            pltpu.SMEM(dest.shape, jnp.int32),
+            pltpu.SMEM(rates.shape, F32),
+            pltpu.VMEM(path_nodes.shape, jnp.int32),
             pltpu.SemaphoreType.DMA((rows,)),
             pltpu.SemaphoreType.DMA((rows,)),
             pltpu.SemaphoreType.DMA((rows,)),
+            pltpu.SemaphoreType.DMA((3,)),
         ],
         compiler_params=pltpu.CompilerParams(vmem_limit_bytes=(49 if direct else 56) << 20),
         cost_estimate=cost(10e6, 5e8),

time: 134 us -> 131 us (0.978)
  Pallas kernels: 40.8 us -> 34.8 us
  blocking collectives: 76.7 us -> 82.3 us
  waiting for transfers between devices: 4.29 us -> 1.38 us
    all_to_all x1, blocking collectives: 76.7 us -> 82.3 us  [swap(): return lax.all_to_all(x, 'req', split_axis=0, concat_axis=0, tiled=True)]
    pallas_call x1, Pallas kernels: 18.5 us -> 14.8 us  [attend(): pl.pallas_call(functools.partial(attend_kernel, rows, width // HD), out_s...]
    all_to_all x1, waiting for transfers between devices: 2.92 us -> 0.01 us  [swap(): return lax.all_to_all(x, 'req', split_axis=0, concat_axis=0, tiled=True)]
  transfers between devices with their start and end apart: 5 -> 5, of which waited for: 2 -> 1; matrix products, arithmetic and copies ran while one was open for 2% -> 2% of each run, Pallas kernels for 19% -> 16%
where the time goes in v3:
time: 131 us; the launch traced here: 130 us
  blocking collectives  82.3 us (63%)
  Pallas kernels  34.8 us (27%)
  starting transfers between devices  8.24 us (6%)
  other arithmetic  2.57 us (2%)
  waiting for transfers between devices  1.38 us (1%)
    all_to_all x1, blocking collectives, swap(): return lax.all_to_all(x, 'req', split_axis=0, concat_axis=0, tiled=True)  82.3 us
    pallas_call x1, Pallas kernels, attend(): pl.pallas_call(functools.partial(attend_kernel, rows, width // HD), out_s...  14.8 us
    pallas_call x2, Pallas kernels, update_states(): pl.pallas_call(functools.partial(update_kernel, rows, first, heads, base)...  12.2 us
    pallas_call x1, Pallas kernels, pack(): pl.pallas_call(functools.partial(pack_kernel, rows, heads), out_shape=(ja...  7.81 us
    ppermute x3, starting transfers between devices, body(): lax.ppermute(square, 'head', [(i, (i + step) % head_count) for i in range...  4.44 us
    all_to_all x1, starting transfers between devices, swap(): return lax.all_to_all(x, 'req', split_axis=0, concat_axis=0, tiled=True)  3.72 us
  transfers between devices with their start and end apart: 5, of which 1 were waited for; matrix products, arithmetic and copies ran while one was open for 2% of the time, Pallas kernels for 16%

profile of v3, /device:TPU:0, one launch (start us, length us, event | category | flops | bytes accessed | tf_op | source)
XLA Modules:
  0.0 130.1 jit_solution(4813945563882468150)
XLA Ops:
  0.6 7.8 %pack.1 = (bf16[16,1552,128]{2,1,0:T(8,128)(2,1)}, bf16[16,512,128]{2,1,0:T(8,128)(2,1)}, s32[16]{0:T(128)}, s32[16]{0:T(128)}) custom-call(s32[1]{0:T(128)} %bitcast.me_ref, s32[256]{0:T(256)} %held_hbm.1, s32[16,64]{1,0:T(8,128)} %parents_hbm.1, s32[16,64]{1,0:T(8,128)} %path_hbm.5, f32[16,1024,128]{2,1,0:T(8,128)} %bitcast.3, ...), custom_call_target="tpu_custom_call" | custom-call | bytes 20000000 | tf_op jit(solution)/shard_map/pack/pallas_call | solution.py:158
  8.5 82.3 %all_to_all.10.early_ref.after_ref.pairs_ref = bf16[16,1552,128]{2,1,0:T(8,128)(2,1)} all-to-all(bf16[16,1552,128]{2,1,0:T(8,128)(2,1)} %get-tuple-element.9), channel_id=1, replica_groups=mesh['req'=16,'head'=8] {'req'}, dimensions={0} | all-to-all | bytes 12713984 | tf_op jit(solution)/shard_map/all_to_all | solution.py:443
  90.8 3.7 %all-to-all-start.1 = ((bf16[16,512,128]{2,1,0:T(8,128)(2,1)}), bf16[16,512,128]{2,1,0:T(8,128)(2,1)S(1)}, u32[]{:S(2)}, u32[]{:S(2)}) async-start(bf16[16,512,128]{2,1,0:T(8,128)(2,1)} %gate.1), calls=%async_computation.1 | async-start | bytes 4194304 | tf_op jit(solution)/shard_map/all_to_all | solution.py:443
  94.5 14.8 %attend.1 = (bf16[16,64,1024]{2,1,0:T(8,128)(2,1)}, f32[16,64]{1,0:T(8,128)}) custom-call(s32[16]{0:T(128)} %get-tuple-element.8.ids_hbm, f32[8]{0:T(128)} %rates_hbm.5, bf16[16,1552,128]{2,1,0:T(8,128)(2,1)} %all_to_all.10.early_ref.after_ref.pairs_ref, bf16[16,64,1024]{2,1,0:T(8,128)(2,1)} %q_hbm.1, bf16[16,64,1024]{2,1,0:T(8,128)(2,1)} %k_hbm.1, ...), custom_call_target="tpu_custom_call" | custom-call | flops 1000000000 | bytes 50000000 | tf_op jit(solution)/shard_map/attend/pallas_call | solution.py:307
  109.3 0.1 collective-permute-start
  109.4 1.4 %collective-permute-done = f32[16,64]{1,0:T(8,128)S(1)} collective-permute-done((f32[16,64]{1,0:T(8,128)}, f32[16,64]{1,0:T(8,128)S(1)}, u32[]{:S(2)}, u32[]{:S(2)}) %collective-permute-start) | collective-permute-done | bytes 4128 | tf_op jit(solution)/shard_map/ppermute | solution.py:453
  110.7 0.7 add.18
  111.4 2.8 %collective-permute-start.3 = (f32[16,64]{1,0:T(8,128)S(1)}, f32[16,64]{1,0:T(8,128)S(1)}, u32[]{:S(2)}, u32[]{:S(2)}) collective-permute-start(f32[16,64]{1,0:T(8,128)S(1)} %add.18), channel_id=1, source_target_pairs={{0,6},{1,7},{2,0},{3,1},{4,2},{5,3},{6,4},{7,5},{8,14},{9,15},{10,... | collective-permute-start | bytes 12296 | tf_op jit(solution)/shard_map/ppermute | solution.py:455
  114.2 0.8 collective-permute-start.2
  115.0 0.9 collective-permute-start.1
  115.9 0.0 copy-start.3
  115.9 0.0 copy-start.4
  115.9 6.5 %update_states.2.refs_0_ = f32[16,1024,128]{2,1,0:T(8,128)} custom-call(s32[16]{0:T(128)} %get-tuple-element.12.dest_hbm, f32[8]{0:T(128)} %rates_hbm.5, s32[16,64]{1,0:T(8,128)} %path_hbm.5, f32[16,1024,128]{2,1,0:T(8,128)} %bitcast.4, bf16[16,1552,128]{2,1,0:T(8,128)(2,1)} %all_to_all.10.early_ref.after_ref.pairs_ref), custom_call_target="tpu_custom_call" | custom-call | flops 500000000 | bytes 10000000 | tf_op jit(solution)/shard_map/update_states/pallas_call | solution.py:409
  122.4 0.0 copy-start
  122.4 0.0 copy-start.1
  122.5 0.0 copy-start.2
  122.5 0.0 collective-permute-done.3
  122.5 0.0 collective-permute-done.2
  122.5 0.0 collective-permute-done.1
  122.5 0.0 copy-done.3
  122.5 0.0 copy-done.4
  122.5 1.9 %multiply_convert_fusion = bf16[16,64,1024]{2,1,0:T(8,128)(2,1)} fusion(bf16[16,64,1024]{2,1,0:T(8,128)(2,1)S(1)} %copy-done.3, f32[1024]{0:T(1024)S(1)} %copy-done.4, f32[16,64]{1,0:T(8,128)S(1)} %add_rsqrt_fusion), kind=kLoop, calls=%fused_computation | loop fusion | flops 4194304 | bytes 4202496 | tf_op jit(solution)/shard_map/convert_element_type | solution.py:460
  124.4 0.0 all-to-all-done.1.pairs_ref
  124.4 0.0 copy-done
  124.4 0.0 copy-done.1
  124.4 0.0 copy-done.2
  124.4 5.6 %update_states.3 = f32[16,1024,128]{2,1,0:T(8,128)} custom-call(s32[16]{0:T(128)S(1)} %copy-done.2, f32[8]{0:T(128)S(1)} %copy-done.1, s32[16,64]{1,0:T(8,128)S(1)} %copy-done, f32[16,1024,128]{2,1,0:T(8,128)} %bitcast.5, bf16[16,512,128]{2,1,0:T(8,128)(2,1)S(1)} %all-to-all-done.1.pairs_ref, ...), custom_call_target="tpu_custom_call", output_to_operand_aliasing={{}: (5, {})} | custom-call | flops 500000000 | bytes 10000000 | tf_op jit(solution)/shard_map/update_states/pallas_call | solution.py:409
  (2 shorter events, 0.0 us)
Async XLA Ops:
  90.8 33.6 %all-to-all-start.1 = ((bf16[16,512,128]{2,1,0:T(8,128)(2,1)}), bf16[16,512,128]{2,1,0:T(8,128)(2,1)S(1)}, u32[]{:S(2)}, u32[]{:S(2)}) async-start(bf16[16,512,128]{2,1,0:T(8,128)(2,1)} %gate.1), calls=%async_computation.1 | async-start | bytes 4194304 | tf_op jit(solution)/shard_map/all_to_all | solution.py:443
  109.3 1.5 %collective-permute-start = (f32[16,64]{1,0:T(8,128)}, f32[16,64]{1,0:T(8,128)S(1)}, u32[]{:S(2)}, u32[]{:S(2)}) collective-permute-start(f32[16,64]{1,0:T(8,128)} %get-tuple-element.11), channel_id=1, source_target_pairs={{0,1},{1,0},{2,3},{3,2},{4,5},{5,4},{6,7},{7,6},{8,9},{9,8},{10,11... | collective-permute-start | bytes 12296 | tf_op jit(solution)/shard_map/ppermute | solution.py:453
  111.4 11.0 %collective-permute-start.3 = (f32[16,64]{1,0:T(8,128)S(1)}, f32[16,64]{1,0:T(8,128)S(1)}, u32[]{:S(2)}, u32[]{:S(2)}) collective-permute-start(f32[16,64]{1,0:T(8,128)S(1)} %add.18), channel_id=1, source_target_pairs={{0,6},{1,7},{2,0},{3,1},{4,2},{5,3},{6,4},{7,5},{8,14},{9,15},{10,... | collective-permute-start | bytes 12296 | tf_op jit(solution)/shard_map/ppermute | solution.py:455
  114.2 8.3 %collective-permute-start.2 = (f32[16,64]{1,0:T(8,128)S(1)}, f32[16,64]{1,0:T(8,128)S(1)}, u32[]{:S(2)}, u32[]{:S(2)}) collective-permute-start(f32[16,64]{1,0:T(8,128)S(1)} %add.18), channel_id=1, source_target_pairs={{0,4},{1,5},{2,6},{3,7},{4,0},{5,1},{6,2},{7,3},{8,12},{9,13},{10,... | collective-permute-start | bytes 12296 | tf_op jit(solution)/shard_map/ppermute | solution.py:455
  115.0 7.5 %collective-permute-start.1 = (f32[16,64]{1,0:T(8,128)S(1)}, f32[16,64]{1,0:T(8,128)S(1)}, u32[]{:S(2)}, u32[]{:S(2)}) collective-permute-start(f32[16,64]{1,0:T(8,128)S(1)} %add.18), channel_id=1, source_target_pairs={{0,2},{1,3},{2,4},{3,5},{4,6},{5,7},{6,0},{7,1},{8,10},{9,11},{10,... | collective-permute-start | bytes 12296 | tf_op jit(solution)/shard_map/ppermute | solution.py:455
  115.9 6.6 %copy-start.3 = (bf16[16,64,1024]{2,1,0:T(8,128)(2,1)S(1)}, bf16[16,64,1024]{2,1,0:T(8,128)(2,1)}, u32[]{:S(2)}) copy-start(bf16[16,64,1024]{2,1,0:T(8,128)(2,1)} %get-tuple-element.10) | copy-start | bytes 6291460
  115.9 6.7 %copy-start.4 = (f32[1024]{0:T(1024)S(1)}, f32[1024]{0:T(1024)}, u32[]{:S(2)}) copy-start(f32[1024]{0:T(1024)} %param.17) | copy-start | bytes 12292
  122.4 2.0 %copy-start = (s32[16,64]{1,0:T(8,128)S(1)}, s32[16,64]{1,0:T(8,128)}, u32[]{:S(2)}) copy-start(s32[16,64]{1,0:T(8,128)} %path_hbm.5) | copy-start | bytes 12292
  122.4 2.0 %copy-start.1 = (f32[8]{0:T(128)S(1)}, f32[8]{0:T(128)}, u32[]{:S(2)}) copy-start(f32[8]{0:T(128)} %rates_hbm.5) | copy-start | bytes 100
  122.5 2.0 %copy-start.2 = (s32[16]{0:T(128)S(1)}, s32[16]{0:T(128)}, u32[]{:S(2)}) copy-start(s32[16]{0:T(128)} %get-tuple-element.12.dest_hbm) | copy-start | bytes 196

commit v4 on v3

--- a/solution.py
+++ b/solution.py
@@ -238,7 +238,7 @@
     col = lax.broadcasted_iota(jnp.int32, (NODES, NODES), 1)
     row_wide = row.astype(F32)
     eye = (row == col).astype(F32)
-    batch = 4
+    batch = rows
 
     def grow(group, carry):
         steps, reaches = [], []

time: 131 us -> 130 us (level)
  Pallas kernels: 34.8 us -> 32 us
  waiting for transfers between devices: 1.38 us -> 3.83 us
    pallas_call x1, Pallas kernels: 14.8 us -> 12 us  [attend(): pl.pallas_call(functools.partial(attend_kernel, rows, width // HD), out_s...]
    all_to_all x1, waiting for transfers between devices: 0.01 us -> 2.45 us  [swap(): return lax.all_to_all(x, 'req', split_axis=0, concat_axis=0, tiled=True)]
  transfers between devices with their start and end apart: 5 -> 5, of which waited for: 1 -> 2; matrix products, arithmetic and copies ran while one was open for 2% -> 2% of each run, Pallas kernels for 16% -> 14%
where the time goes in v4:
time: 130 us
  blocking collectives  82.3 us (63%)
  Pallas kernels  32 us (25%)
  starting transfers between devices  8.23 us (6%)
  waiting for transfers between devices  3.83 us (3%)
  other arithmetic  2.57 us (2%)
    all_to_all x1, blocking collectives, swap(): return lax.all_to_all(x, 'req', split_axis=0, concat_axis=0, tiled=True)  82.3 us
    pallas_call x2, Pallas kernels, update_states(): pl.pallas_call(functools.partial(update_kernel, rows, first, heads, base)...  12.2 us
    pallas_call x1, Pallas kernels, attend(): pl.pallas_call(functools.partial(attend_kernel, rows, width // HD), out_s...  12 us
    pallas_call x1, Pallas kernels, pack(): pl.pallas_call(functools.partial(pack_kernel, rows, heads), out_shape=(ja...  7.8 us
    ppermute x3, starting transfers between devices, body(): lax.ppermute(square, 'head', [(i, (i + step) % head_count) for i in range...  4.43 us
    all_to_all x1, starting transfers between devices, swap(): return lax.all_to_all(x, 'req', split_axis=0, concat_axis=0, tiled=True)  3.72 us
  transfers between devices with their start and end apart: 5, of which 2 were waited for; matrix products, arithmetic and copies ran while one was open for 2% of the time, Pallas kernels for 14%

profile of v4, /device:TPU:0, one launch (start us, length us, event | category | flops | bytes accessed | tf_op | source)
XLA Modules:
  0.0 129.7 jit_solution(5598310274780528592)
XLA Ops:
  0.6 7.8 %pack.1 = (bf16[16,1552,128]{2,1,0:T(8,128)(2,1)}, bf16[16,512,128]{2,1,0:T(8,128)(2,1)}, s32[16]{0:T(128)}, s32[16]{0:T(128)}) custom-call(s32[1]{0:T(128)} %bitcast.me_ref, s32[256]{0:T(256)} %held_hbm.1, s32[16,64]{1,0:T(8,128)} %parents_hbm.1, s32[16,64]{1,0:T(8,128)} %path_hbm.5, f32[16,1024,128]{2,1,0:T(8,128)} %bitcast.3, ...), custom_call_target="tpu_custom_call" | custom-call | bytes 20000000 | tf_op jit(solution)/shard_map/pack/pallas_call | solution.py:158
  8.4 82.3 %all_to_all.10.early_ref.after_ref.pairs_ref = bf16[16,1552,128]{2,1,0:T(8,128)(2,1)} all-to-all(bf16[16,1552,128]{2,1,0:T(8,128)(2,1)} %get-tuple-element.9), channel_id=1, replica_groups=mesh['req'=16,'head'=8] {'req'}, dimensions={0} | all-to-all | bytes 12713984 | tf_op jit(solution)/shard_map/all_to_all | solution.py:443
  90.8 3.7 %all-to-all-start.1 = ((bf16[16,512,128]{2,1,0:T(8,128)(2,1)}), bf16[16,512,128]{2,1,0:T(8,128)(2,1)S(1)}, u32[]{:S(2)}, u32[]{:S(2)}) async-start(bf16[16,512,128]{2,1,0:T(8,128)(2,1)} %gate.1), calls=%async_computation.1 | async-start | bytes 4194304 | tf_op jit(solution)/shard_map/all_to_all | solution.py:443
  94.5 12.0 %attend.1 = (bf16[16,64,1024]{2,1,0:T(8,128)(2,1)}, f32[16,64]{1,0:T(8,128)}) custom-call(s32[16]{0:T(128)} %get-tuple-element.8.ids_hbm, f32[8]{0:T(128)} %rates_hbm.5, bf16[16,1552,128]{2,1,0:T(8,128)(2,1)} %all_to_all.10.early_ref.after_ref.pairs_ref, bf16[16,64,1024]{2,1,0:T(8,128)(2,1)} %q_hbm.1, bf16[16,64,1024]{2,1,0:T(8,128)(2,1)} %k_hbm.1, ...), custom_call_target="tpu_custom_call" | custom-call | flops 1000000000 | bytes 50000000 | tf_op jit(solution)/shard_map/attend/pallas_call | solution.py:307
  106.5 0.1 collective-permute-start
  106.6 1.4 %collective-permute-done = f32[16,64]{1,0:T(8,128)S(1)} collective-permute-done((f32[16,64]{1,0:T(8,128)}, f32[16,64]{1,0:T(8,128)S(1)}, u32[]{:S(2)}, u32[]{:S(2)}) %collective-permute-start) | collective-permute-done | bytes 4128 | tf_op jit(solution)/shard_map/ppermute | solution.py:453
  108.0 0.7 add.18
  108.7 2.7 %collective-permute-start.3 = (f32[16,64]{1,0:T(8,128)S(1)}, f32[16,64]{1,0:T(8,128)S(1)}, u32[]{:S(2)}, u32[]{:S(2)}) collective-permute-start(f32[16,64]{1,0:T(8,128)S(1)} %add.18), channel_id=1, source_target_pairs={{0,6},{1,7},{2,0},{3,1},{4,2},{5,3},{6,4},{7,5},{8,14},{9,15},{10,... | collective-permute-start | bytes 12296 | tf_op jit(solution)/shard_map/ppermute | solution.py:455
  111.4 0.8 collective-permute-start.2
  112.2 0.9 collective-permute-start.1
  113.1 0.0 copy-start.3
  113.1 0.0 copy-start.4
  113.1 6.5 %update_states.2.refs_0_ = f32[16,1024,128]{2,1,0:T(8,128)} custom-call(s32[16]{0:T(128)} %get-tuple-element.12.dest_hbm, f32[8]{0:T(128)} %rates_hbm.5, s32[16,64]{1,0:T(8,128)} %path_hbm.5, f32[16,1024,128]{2,1,0:T(8,128)} %bitcast.4, bf16[16,1552,128]{2,1,0:T(8,128)(2,1)} %all_to_all.10.early_ref.after_ref.pairs_ref), custom_call_target="tpu_custom_call" | custom-call | flops 500000000 | bytes 10000000 | tf_op jit(solution)/shard_map/update_states/pallas_call | solution.py:409
  119.7 0.0 copy-start
  119.7 0.0 copy-start.1
  119.7 0.0 copy-start.2
  119.7 0.0 collective-permute-done.3
  119.7 0.0 collective-permute-done.2
  119.7 0.0 collective-permute-done.1
  119.7 0.0 copy-done.3
  119.7 0.0 copy-done.4
  119.8 1.9 %multiply_convert_fusion = bf16[16,64,1024]{2,1,0:T(8,128)(2,1)} fusion(bf16[16,64,1024]{2,1,0:T(8,128)(2,1)S(1)} %copy-done.3, f32[1024]{0:T(1024)S(1)} %copy-done.4, f32[16,64]{1,0:T(8,128)S(1)} %add_rsqrt_fusion), kind=kLoop, calls=%fused_computation | loop fusion | flops 4194304 | bytes 4202496 | tf_op jit(solution)/shard_map/convert_element_type | solution.py:460
  121.6 2.5 %all-to-all-done.1.pairs_ref = bf16[16,512,128]{2,1,0:T(8,128)(2,1)S(1)} async-done(((bf16[16,512,128]{2,1,0:T(8,128)(2,1)}), bf16[16,512,128]{2,1,0:T(8,128)(2,1)S(1)}, u32[]{:S(2)}, u32[]{:S(2)}) %all-to-all-start.1) | async-done | bytes 2097184 | tf_op jit(solution)/shard_map/all_to_all | solution.py:443
  124.1 0.0 copy-done
  124.1 0.0 copy-done.1
  124.1 0.0 copy-done.2
  124.1 5.6 %update_states.3 = f32[16,1024,128]{2,1,0:T(8,128)} custom-call(s32[16]{0:T(128)S(1)} %copy-done.2, f32[8]{0:T(128)S(1)} %copy-done.1, s32[16,64]{1,0:T(8,128)S(1)} %copy-done, f32[16,1024,128]{2,1,0:T(8,128)} %bitcast.5, bf16[16,512,128]{2,1,0:T(8,128)(2,1)S(1)} %all-to-all-done.1.pairs_ref, ...), custom_call_target="tpu_custom_call", output_to_operand_aliasing={{}: (5, {})} | custom-call | flops 500000000 | bytes 10000000 | tf_op jit(solution)/shard_map/update_states/pallas_call | solution.py:409
  (2 shorter events, 0.0 us)
Async XLA Ops:
  90.8 33.3 %all-to-all-start.1 = ((bf16[16,512,128]{2,1,0:T(8,128)(2,1)}), bf16[16,512,128]{2,1,0:T(8,128)(2,1)S(1)}, u32[]{:S(2)}, u32[]{:S(2)}) async-start(bf16[16,512,128]{2,1,0:T(8,128)(2,1)} %gate.1), calls=%async_computation.1 | async-start | bytes 4194304 | tf_op jit(solution)/shard_map/all_to_all | solution.py:443
  106.5 1.5 %collective-permute-start = (f32[16,64]{1,0:T(8,128)}, f32[16,64]{1,0:T(8,128)S(1)}, u32[]{:S(2)}, u32[]{:S(2)}) collective-permute-start(f32[16,64]{1,0:T(8,128)} %get-tuple-element.11), channel_id=1, source_target_pairs={{0,1},{1,0},{2,3},{3,2},{4,5},{5,4},{6,7},{7,6},{8,9},{9,8},{10,11... | collective-permute-start | bytes 12296 | tf_op jit(solution)/shard_map/ppermute | solution.py:453
  108.7 11.0 %collective-permute-start.3 = (f32[16,64]{1,0:T(8,128)S(1)}, f32[16,64]{1,0:T(8,128)S(1)}, u32[]{:S(2)}, u32[]{:S(2)}) collective-permute-start(f32[16,64]{1,0:T(8,128)S(1)} %add.18), channel_id=1, source_target_pairs={{0,6},{1,7},{2,0},{3,1},{4,2},{5,3},{6,4},{7,5},{8,14},{9,15},{10,... | collective-permute-start | bytes 12296 | tf_op jit(solution)/shard_map/ppermute | solution.py:455
  111.4 8.3 %collective-permute-start.2 = (f32[16,64]{1,0:T(8,128)S(1)}, f32[16,64]{1,0:T(8,128)S(1)}, u32[]{:S(2)}, u32[]{:S(2)}) collective-permute-start(f32[16,64]{1,0:T(8,128)S(1)} %add.18), channel_id=1, source_target_pairs={{0,4},{1,5},{2,6},{3,7},{4,0},{5,1},{6,2},{7,3},{8,12},{9,13},{10,... | collective-permute-start | bytes 12296 | tf_op jit(solution)/shard_map/ppermute | solution.py:455
  112.2 7.5 %collective-permute-start.1 = (f32[16,64]{1,0:T(8,128)S(1)}, f32[16,64]{1,0:T(8,128)S(1)}, u32[]{:S(2)}, u32[]{:S(2)}) collective-permute-start(f32[16,64]{1,0:T(8,128)S(1)} %add.18), channel_id=1, source_target_pairs={{0,2},{1,3},{2,4},{3,5},{4,6},{5,7},{6,0},{7,1},{8,10},{9,11},{10,... | collective-permute-start | bytes 12296 | tf_op jit(solution)/shard_map/ppermute | solution.py:455
  113.1 6.6 %copy-start.3 = (bf16[16,64,1024]{2,1,0:T(8,128)(2,1)S(1)}, bf16[16,64,1024]{2,1,0:T(8,128)(2,1)}, u32[]{:S(2)}) copy-start(bf16[16,64,1024]{2,1,0:T(8,128)(2,1)} %get-tuple-element.10) | copy-start | bytes 6291460
  113.1 6.7 %copy-start.4 = (f32[1024]{0:T(1024)S(1)}, f32[1024]{0:T(1024)}, u32[]{:S(2)}) copy-start(f32[1024]{0:T(1024)} %param.17) | copy-start | bytes 12292
  119.7 4.4 %copy-start = (s32[16,64]{1,0:T(8,128)S(1)}, s32[16,64]{1,0:T(8,128)}, u32[]{:S(2)}) copy-start(s32[16,64]{1,0:T(8,128)} %path_hbm.5) | copy-start | bytes 12292
  119.7 4.4 %copy-start.1 = (f32[8]{0:T(128)S(1)}, f32[8]{0:T(128)}, u32[]{:S(2)}) copy-start(f32[8]{0:T(128)} %rates_hbm.5) | copy-start | bytes 100
  119.7 4.4 %copy-start.2 = (s32[16]{0:T(128)S(1)}, s32[16]{0:T(128)}, u32[]{:S(2)}) copy-start(s32[16]{0:T(128)} %get-tuple-element.12.dest_hbm) | copy-start | bytes 196
